TPU v7x, 32 devices: a whole 2x2x4 slice. The times are simulated.
32 devices in a mesh: dp: 4 (over y, x), ctx: 8 (over z, core).
Axes of the slice: x: 2, y: 2, z: 4, core: 2. Of those that a mesh axis runs over, the one named last changes fastest.
Arguments:
- patches: bfloat16 [4, 640, 1024], P('dp', 'ctx'), may hold values from -6 to 6
- vis_index: int32 [4, 640], P('dp', 'ctx'), may hold values from 0 to 784, as said below
- shifts: int32 [4, 3], P('dp'), may hold values from 0 to 6, as said below
- enc_gain: float32 [1024], replicated, may hold values from 0.5 to 1.5
- enc_qkv: bfloat16 [1024, 1536], replicated, may hold values from -64 to 64, as said below
- enc_out: bfloat16 [512, 1024], replicated, may hold values from -0.25 to 0.25
- enc_to_dec: bfloat16 [1024, 512], replicated, may hold values from -0.1875 to 0.1875
- mask_token: float32 [512], replicated, may hold values from -6 to 6
- dec_gain: float32 [512], replicated, may hold values from 0.5 to 1.5
- dec_qkv: bfloat16 [512, 768], replicated, may hold values from -64 to 64, as said below
- dec_out: bfloat16 [256, 512], replicated, may hold values from -0.375 to 0.375
- dec_cot: bfloat16 [4, 6272, 512], P('dp', 'ctx'), may hold values from -6 to 6
Outputs:
- d_patches: bfloat16 [4, 640, 1024], P('dp', 'ctx')
- grad_flat: float32 [3147776], P(('dp', 'ctx'))
Inputs may be any that keep to these rules, and one draw needn't show every extreme that they name: `vis_index`: slots j * 80 to (j + 1) * 80 - 1 of a clip belong to time shard j; its live values are distinct token positions of the shard and stand first, the other slots hold 784. Every shard has 40 or more live slots, and every clip has a shard whose 80 slots are all live. `shifts`: column 0 is the offset in time, below 4; columns 1 and 2 are the offsets along rows and columns, below 7. One clip has offsets 3, 6, 6 and another 0, 0, 0. `enc_qkv`: entries of the size of the inverse square root of the input width. `dec_qkv`: entries of the size of the inverse square root of the input width.
All inputs are finite; a program needn't handle non-finite values.
Results may differ from a plain program's by a relative error of at most 0.02.
Values may be sent and summed in bfloat16 or wider, within the bound.
No kernel may reach another device: no remote copies, remote signals or barrier semaphores. Data moves between devices by JAX's collectives and lax.ppermute only.
A program may use at most 128 MiB of HBM per device.

v0:
```python
import jax
import jax.numpy as jnp
from jax import lax
from jax.sharding import PartitionSpec as P

HEAD = 64
WT = 4
GRID = 14
SW = 7


norm_eps = 1e-06


def extended(block, sides, width):
    for axis, dim in sides:
        count = lax.axis_size(axis)
        forward = [(i, i + 1) for i in range(count - 1)]
        forward.append((count - 1, 0))
        backward = [(target, source) for source, target in forward]
        low = lax.ppermute(
            lax.slice_in_dim(block, block.shape[dim] - width, None, axis=dim), axis, forward
        )
        high = lax.ppermute(lax.slice_in_dim(block, 0, width, axis=dim), axis, backward)
        block = jnp.concatenate([low, block, high], axis=dim)
    return block


def layer_norm(inputs, gain):
    values = inputs.astype(jnp.float32)
    center = values - jnp.mean(values, axis=-1, keepdims=True)
    spread = jnp.mean(center * center, axis=-1, keepdims=True)
    return (center * lax.rsqrt(spread + norm_eps) * gain).astype(jnp.bfloat16)


def softmax_rows(scores):
    highest = jnp.max(scores, axis=-1, keepdims=True)
    raised = jnp.exp(scores - highest)
    return (raised / jnp.sum(raised, axis=-1, keepdims=True)).astype(jnp.bfloat16)


def enc_project(inputs, gain, weight):
    normed = layer_norm(inputs, gain)
    joined = jnp.dot(normed, weight, preferred_element_type=jnp.float32).astype(jnp.bfloat16)
    channels = weight.shape[1] // 3
    return (joined[:, :channels], joined[:, channels : 2 * channels], joined[:, 2 * channels :])


def enc_attend(query, key_all, value_all, live_all):
    query_rows = query.shape[0]
    key_rows = key_all.shape[0]
    head_count = query.shape[1] // HEAD
    query_heads = query.reshape(query_rows, head_count, HEAD).transpose(1, 0, 2)
    key_heads = key_all.reshape(key_rows, head_count, HEAD).transpose(1, 0, 2)
    value_heads = value_all.reshape(key_rows, head_count, HEAD).transpose(1, 0, 2)
    scores = jnp.einsum(
        "hrd,hkd->hrk", query_heads, key_heads, preferred_element_type=jnp.float32
    ) * HEAD ** (-0.5)
    scores = jnp.where(live_all[None, None, :] > 0.5, scores, -1e30)
    weights = softmax_rows(scores)
    mixed = jnp.einsum("hrk,hkd->hrd", weights, value_heads, preferred_element_type=jnp.float32)
    return mixed.transpose(1, 0, 2).reshape(query_rows, -1).astype(jnp.bfloat16)


def enc_finish(inputs, mixed, out_weight, down_weight):
    residual = (
        inputs.astype(jnp.float32) + jnp.dot(mixed, out_weight, preferred_element_type=jnp.float32)
    ).astype(jnp.bfloat16)
    return jnp.dot(residual, down_weight, preferred_element_type=jnp.float32).astype(jnp.bfloat16)


def build_grid(latent, slot_index, token, token_rows):
    base = jnp.broadcast_to(token, (token_rows, token.shape[0]))
    return base.at[slot_index].set(latent.astype(jnp.float32), mode="drop").astype(jnp.bfloat16)


def dec_project(dec_grid, gain, weight):
    normed = layer_norm(dec_grid, gain)
    joined = jnp.dot(normed, weight, preferred_element_type=jnp.float32).astype(jnp.bfloat16)
    channels = weight.shape[1] // 3
    return (joined[:, :channels], joined[:, channels:])


def dec_mix(query, pair_ext, dec_grid, offsets, weight):
    cell_count = GRID * GRID
    steps_own = query.shape[0] // cell_count
    channels = query.shape[1]
    window_span = steps_own + WT
    query_ext = jnp.pad(query.reshape(steps_own, cell_count, channels), ((WT, WT), (0, 0), (0, 0)))
    offset = (offsets[0] + WT - 1) % WT + 1 - WT
    slice_start = offset + WT
    query_win = lax.dynamic_slice_in_dim(query_ext, slice_start, window_span, 0)
    pair_win = lax.dynamic_slice_in_dim(pair_ext, slice_start, window_span, 0)
    joined = jnp.concatenate([query_win, pair_win], -1).reshape(
        window_span, GRID, GRID, 3 * channels
    )
    joined = jnp.roll(joined, (-offsets[1], -offsets[2]), axis=(1, 2))
    side_count = GRID // SW
    windows = joined.reshape(window_span // WT, WT, side_count, SW, side_count, SW, 3 * channels)
    windows = windows.transpose(0, 2, 4, 1, 3, 5, 6).reshape(-1, WT * SW * SW, 3 * channels)
    head_count = channels // HEAD
    window_count = windows.shape[0]
    token_count = windows.shape[1]
    query_heads = (
        windows[..., :channels]
        .reshape(window_count, token_count, head_count, HEAD)
        .transpose(0, 2, 1, 3)
    )
    key_heads = (
        windows[..., channels : 2 * channels]
        .reshape(window_count, token_count, head_count, HEAD)
        .transpose(0, 2, 1, 3)
    )
    value_heads = (
        windows[..., 2 * channels :]
        .reshape(window_count, token_count, head_count, HEAD)
        .transpose(0, 2, 1, 3)
    )
    scores = jnp.einsum(
        "nhqd,nhkd->nhqk", query_heads, key_heads, preferred_element_type=jnp.float32
    ) * HEAD ** (-0.5)
    weights = softmax_rows(scores)
    attended = jnp.einsum(
        "nhqk,nhkd->nhqd", weights, value_heads, preferred_element_type=jnp.float32
    ).astype(jnp.bfloat16)
    attended = attended.transpose(0, 2, 1, 3)
    attended = attended.reshape(window_span // WT, side_count, side_count, WT, SW, SW, channels)
    attended = attended.transpose(0, 3, 1, 4, 2, 5, 6).reshape(window_span, GRID, GRID, channels)
    attended = jnp.roll(attended, (offsets[1], offsets[2]), axis=(1, 2)).reshape(
        window_span, cell_count, channels
    )
    own_rows = lax.dynamic_slice_in_dim(attended, -offset, steps_own, 0).reshape(-1, channels)
    return dec_grid.astype(jnp.float32) + jnp.dot(
        own_rows, weight, preferred_element_type=jnp.float32
    )


def assemble(middle, from_left, from_right):
    total = middle.astype(jnp.float32)
    total = total + from_left.astype(jnp.float32)
    total = total + from_right.astype(jnp.float32)
    return total.astype(jnp.bfloat16)


def flatten(members):
    joined = jnp.concatenate([member.astype(jnp.float32).reshape(-1) for member in members])
    return joined


def body(
    patches,
    vis_index,
    shifts,
    enc_gain,
    enc_qkv,
    enc_out,
    enc_to_dec,
    mask_token,
    dec_gain,
    dec_qkv,
    dec_out,
    dec_cot,
):
    tokens = patches[0]
    slot_index = vis_index[0]
    offsets = shifts[0]
    token_rows = dec_cot.shape[1]
    cell_count = GRID * GRID
    steps_own = token_rows // cell_count
    live_own = (slot_index < token_rows).astype(jnp.bfloat16)
    (query, key_own, value_own), project_pull = jax.vjp(enc_project, tokens, enc_gain, enc_qkv)
    key_all, value_all, live_all = (
        lax.all_gather(key_own, "ctx", axis=0, tiled=True),
        lax.all_gather(value_own, "ctx", axis=0, tiled=True),
        lax.all_gather(live_own, "ctx", axis=0, tiled=True),
    )

    def attend_fn(first, second, third):
        return enc_attend(first, second, third, live_all)

    mixed, attend_pull = jax.vjp(attend_fn, query, key_all, value_all)
    latent, finish_pull = jax.vjp(enc_finish, tokens, mixed, enc_out, enc_to_dec)

    def grid_fn(first, second):
        return build_grid(first, slot_index, second, token_rows)

    dec_grid, grid_pull = jax.vjp(grid_fn, latent, mask_token)
    (dec_query, dec_pair), dproj_pull = jax.vjp(dec_project, dec_grid, dec_gain, dec_qkv)
    pair_cube = dec_pair.reshape(steps_own, cell_count, dec_pair.shape[1])
    pair_ext = extended(pair_cube, (("ctx", 0),), WT)

    def mix_fn(first, second, third, fourth):
        return dec_mix(first, second, third, offsets, fourth)

    decoded, mix_pull = jax.vjp(mix_fn, dec_query, pair_ext, dec_grid, dec_out)
    d_query, d_ext, d_grid_mix, d_dout = mix_pull(dec_cot[0].astype(jnp.float32))
    rim_grads = jnp.concatenate([d_ext[:WT], d_ext[steps_own + WT :]], 0)
    beside_all = extended(rim_grads, (("ctx", 0),), WT)
    from_left = beside_all[:WT]
    from_right = beside_all[3 * WT :]
    d_pair = assemble(d_ext[WT : steps_own + WT], from_left, from_right).reshape(token_rows, -1)
    d_grid_proj, d_dgain, d_dqkv = dproj_pull((d_query, d_pair))
    d_grid = (d_grid_mix.astype(jnp.float32) + d_grid_proj.astype(jnp.float32)).astype(jnp.bfloat16)
    d_latent, d_mask = grid_pull(d_grid)
    d_tokens_res, d_mixed, d_eout, d_e2d = finish_pull(d_latent)
    d_query_enc, d_key_all, d_value_all = attend_pull(d_mixed)
    d_key, d_value = (
        lax.psum_scatter(
            d_key_all.astype(jnp.float32).astype(jnp.bfloat16),
            "ctx",
            scatter_dimension=0,
            tiled=True,
        ).astype(jnp.float32),
        lax.psum_scatter(
            d_value_all.astype(jnp.float32).astype(jnp.bfloat16),
            "ctx",
            scatter_dimension=0,
            tiled=True,
        ).astype(jnp.float32),
    )
    d_tokens_proj, d_egain, d_eqkv = project_pull(
        (d_query_enc, d_key.astype(jnp.bfloat16), d_value.astype(jnp.bfloat16))
    )
    d_patches = (d_tokens_res.astype(jnp.float32) + d_tokens_proj.astype(jnp.float32)).astype(
        jnp.bfloat16
    )[None]
    flat_grads = flatten((d_egain, d_eqkv, d_eout, d_e2d, d_mask, d_dgain, d_dqkv, d_dout))
    clip_share = lax.psum_scatter(
        flat_grads.astype(jnp.bfloat16), "dp", scatter_dimension=0, tiled=True
    )
    summed = lax.psum_scatter(clip_share, "ctx", scatter_dimension=0, tiled=True).astype(
        jnp.float32
    )
    return (d_patches, summed)


def solution(mesh):
    in_specs = (
        P("dp", "ctx", None),
        P("dp", "ctx"),
        P("dp", None),
        P(),
        P(),
        P(),
        P(),
        P(),
        P(),
        P(),
        P(),
        P("dp", "ctx", None),
    )
    out_specs = (P("dp", "ctx", None), P(("dp", "ctx")))
    return jax.shard_map(body, mesh=mesh, in_specs=in_specs, out_specs=out_specs, check_vma=False)
```

profile of v0, /device:TPU:0, one launch (start us, length us, event | category | flops | bytes accessed | tf_op | source)
XLA Modules:
  0.0 607.7 jit_solution(16050429970419509778)
XLA Ops:
  13.7 17.9 %all_gather.10 = bf16[640,512]{1,0:T(8,128)(2,1)} all-gather(bf16[80,512]{1,0:T(8,128)(2,1)S(1)} %get-tuple-element.27), channel_id=1, replica_groups=mesh['dp'=4,'ctx'=8] {'ctx'}, dimensions={0}, use_global_device_ids=true | all-gather | bytes 737280 | tf_op jit(solution)/shard_map/all_gather | solution.py:173
  35.4 16.8 %all-reduce.9 = bf16[640]{0:T(1024)(128)(2,1)S(1)} all-reduce(bf16[640]{0:T(1024)(128)(2,1)S(1)} %dynamic-update-slice), channel_id=1, replica_groups=mesh['dp'=4,'ctx'=8] {'ctx'}, use_global_device_ids=true, to_apply=%add.9 | all-reduce | flops 640 | bytes 2560
  55.8 16.2 %all_gather.11 = bf16[640,512]{1,0:T(8,128)(2,1)} all-gather(bf16[80,512]{1,0:T(8,128)(2,1)S(1)} %get-tuple-element.26), channel_id=1, replica_groups=mesh['dp'=4,'ctx'=8] {'ctx'}, dimensions={0}, use_global_device_ids=true | all-gather | bytes 737280 | tf_op jit(solution)/shard_map/all_gather | solution.py:174
  84.2 3.6 scatter_fusion
  115.8 9.7 %dynamic_update_slice.25 = bf16[8,196,256]{2,0,1:T(8,128)(2,1)} dynamic-update-slice(bf16[8,196,256]{2,0,1:T(8,128)(2,1)} %broadcast_in_dim.105, bf16[4,196,256]{2,0,1:T(4,128)(2,1)} %copy.60, s32[]{:T(128)S(6)} %select_n.105, s32[]{:T(128)} %constant.119.clone.1, s32[]{:T(128)} %constant.119.clone.1) | dynamic-update-slice | bytes 802820 | tf_op jit(solution)/shard_map/transpose(jvp())/dynamic_update_slice | solution.py:132
  133.1 4.3 reshape.276
  137.3 3.9 copy.63
  150.4 5.3 reshape.269
  155.7 5.1 copy.57
  160.7 6.6 %reshape.270 = bf16[8,196,768]{2,0,1:T(8,128)(2,1)} reshape(bf16[2,2,2,4,7,7,768]{6,2,1,0,5,4,3:T(2,128)(2,1)} %copy.57) | data formatting | bytes 4816896 | tf_op jit(solution)/shard_map/jvp()/reshape | solution.py:100
  182.9 7.2 %convert_reduce_fusion = (f32[8,4,196]{2,1,0:T(4,128)S(1)}, pred[8,4,196,196]{2,3,1,0:T(8,128)(4,1)S(1)}, f32[8,4,196]{2,1,0:T(4,128)S(1)}, bf16[8,4,196,196]{2,3,1,0:T(8,128)(2,1)S(1)}) fusion(f32[8,4,196]{2,1,0:T(4,128)S(1)} %get-tuple-element.38, f32[8,4,196,196]{2,3,1,0:T(8,128)} %copy-done.1, f32[8,4,196]{2,1,0:T(4,128)S(1)} %multiply_divide_fusion, ...), kind=kOutput, calls=%fused_computation.11 | convolution fusion | flops 169632512 | bytes 10311168 | tf_op jit(solution)/shard_map/transpose(jvp(nhqk,nhkd->nhqd))/dot_general | solution.py:123
  210.5 6.1 reshape.281
  216.5 4.0 copy.71
  220.5 5.1 reshape.282
  233.3 17.6 %dynamic_update_slice.30 = bf16[12,196,512]{2,0,1:T(8,128)(2,1)} dynamic-update-slice(bf16[12,196,512]{2,0,1:T(8,128)(2,1)} %broadcast_in_dim.97, bf16[8,196,512]{2,0,1:T(8,128)(2,1)} %split.56, s32[]{:T(128)S(6)} %select_n.100, s32[]{:T(128)} %constant.119.clone.1, s32[]{:T(128)} %constant.119.clone.1) | dynamic-update-slice | bytes 3211268 | tf_op jit(solution)/shard_map/transpose(jvp())/dynamic_update_slice | solution.py:93
  250.9 3.6 fusion.99
  260.9 3.9 fusion.36
  264.8 4.3 copy.77
  269.1 4.0 reshape.294
  338.8 30.1 %reduce-scatter.9.cloned.1.call-done = bf16[80,512]{1,0:T(8,128)(2,1)} async-done(((bf16[640,512]{1,0:T(8,128)(2,1)}), bf16[80,512]{1,0:T(8,128)(2,1)}) %reduce-scatter.9.cloned.1.call-update) | async-done | bytes 81936
  370.6 3.9 convolution_convert_fusion
  376.4 6.9 %reshape.290 = bf16[1572864]{0:T(1024)(128)(2,1)} reshape(bf16[1024,1536]{1,0:T(8,128)(2,1)} %convolution_convert_fusion) | data formatting | bytes 6291456 | tf_op jit(solution)/shard_map/reshape | solution.py:146
  398.5 135.3 %all-reduce.15.cloned.1.call-done = bf16[3147776]{0:T(1024)(128)(2,1)} async-done(((bf16[3147776]{0:T(1024)(128)(2,1)}), bf16[3147776]{0:T(1024)(128)(2,1)}) %all-reduce.15.cloned.1.call-update) | async-done | bytes 6295568
  539.7 59.2 %all-reduce.17.cloned.1.call-done = bf16[786944]{0:T(1024)(128)(2,1)} async-done(((bf16[786944]{0:T(1024)(128)(2,1)}), bf16[786944]{0:T(1024)(128)(2,1)}) %all-reduce.17.cloned.1.call-update) | async-done | bytes 1573904
  (322 shorter events, 206.7 us)
Async XLA Ops:
  7.2 4.9 copy-start
  7.2 329.9 %reduce-scatter.7.cloned.1.call-start = ((), (), s32[]{:S(2)}) async-start(), calls=%async_computation.2 | async-start | bytes 737280
  13.7 20.3 %copy-start.74 = (u32[32]{0:T(128)S(1)}, u32[32]{0:T(128)}, u32[]{:S(2)}) copy-start(u32[32]{0:T(128)} %constant.167) | copy-start | bytes 388
  33.9 20.6 %copy-start.38 = (bf16[80,512]{0,1:T(8,128)(2,1)}, bf16[80,512]{0,1:T(8,128)(2,1)S(1)}, u32[]{:S(2)}) copy-start(bf16[80,512]{0,1:T(8,128)(2,1)S(1)} %copy.84) | copy-start | bytes 245764
  54.5 87.9 %copy-start.48 = (f32[8,80]{1,0:T(8,128)}, f32[8,80]{1,0:T(8,128)S(1)}, u32[]{:S(2)}) copy-start(f32[8,80]{1,0:T(8,128)S(1)} %fusion.42) | copy-start | bytes 7684
  78.7 4.8 copy-start.36
  89.6 201.3 %copy-start.51 = (f32[784]{0:T(1024)}, f32[784]{0:T(1024)S(1)}, u32[]{:S(2)}) copy-start(f32[784]{0:T(1024)S(1)} %broadcast_multiply_fusion) | copy-start | bytes 9412
  90.0 200.8 %copy-start.53 = (f32[784]{0:T(1024)}, f32[784]{0:T(1024)S(1)}, u32[]{:S(2)}) copy-start(f32[784]{0:T(1024)S(1)} %fusion.73) | copy-start | bytes 9412
  92.9 8.2 %copy-start.64 = (s32[1,3]{1,0:T(1,128)S(1)}, s32[1,3]{1,0:T(1,128)}, u32[]{:S(2)}) copy-start(s32[1,3]{1,0:T(1,128)} %param.14) | copy-start | bytes 40
  97.6 45.5 %collective-permute-start = (bf16[4,196,512]{2,0,1:T(4,128)(2,1)}, bf16[4,196,512]{2,0,1:T(4,128)(2,1)}, u32[]{:S(2)}, u32[]{:S(2)}) collective-permute-start(bf16[4,196,512]{2,0,1:T(4,128)(2,1)} %copy.52), channel_id=1, source_target_pairs={{0,1},{1,2},{2,3},{3,4},{4,5},{5,6},{6,7},{7,0},{8,9},{9,10},{10,1... | collective-permute-start | bytes 2408456 | tf_op jit(solution)/shard_map/ppermute | solution.py:21
  97.9 46.4 %collective-permute-start.1 = (bf16[4,196,512]{2,0,1:T(4,128)(2,1)}, bf16[4,196,512]{2,0,1:T(4,128)(2,1)}, u32[]{:S(2)}, u32[]{:S(2)}) collective-permute-start(bf16[4,196,512]{2,0,1:T(4,128)(2,1)} %copy.52), channel_id=1, source_target_pairs={{1,0},{2,1},{3,2},{4,3},{5,4},{6,5},{7,6},{0,7},{9,8},{10,9},{11,1... | collective-permute-start | bytes 2408456 | tf_op jit(solution)/shard_map/ppermute | solution.py:24
  182.9 7.2 %slice-start = ((s8[6553600]{0:T(1024)(128)(4,1)}), s8[4194304]{0:T(1024)(128)(4,1)S(1)}, s32[]{:S(2)}) async-start(s8[6553600]{0:T(1024)(128)(4,1)} %bitcast.179), calls=%async_computation.6 | async-start | bytes 8388608
  182.9 7.2 %slice-start.1 = ((s8[6553600]{0:T(1024)(128)(4,1)}), s8[2359296]{0:T(1024)(128)(4,1)S(1)}, s32[]{:S(2)}) async-start(s8[6553600]{0:T(1024)(128)(4,1)} %bitcast.179), calls=%async_computation.7 | async-start | bytes 4718592
  192.9 5.0 copy-start.5
  250.9 7.2 %copy-start.23 = (bf16[8,196,256]{2,0,1:T(8,128)(2,1)S(1)}, bf16[8,196,256]{2,0,1:T(8,128)(2,1)}, u32[]{:S(2)}) copy-start(bf16[8,196,256]{2,0,1:T(8,128)(2,1)} %split.57) | copy-start | bytes 2408452
  254.4 26.0 %collective-permute-start.2 = (bf16[4,196,512]{2,0,1:T(4,128)(2,1)}, bf16[4,196,512]{2,0,1:T(4,128)(2,1)}, u32[]{:S(2)}, u32[]{:S(2)}) collective-permute-start(bf16[4,196,512]{2,0,1:T(4,128)(2,1)} %get-tuple-element.20), channel_id=1, source_target_pairs={{0,1},{1,2},{2,3},{3,4},{4,5},{5,6},{6,7},{7,0},{8,9},{9,10},{10,1... | collective-permute-start | bytes 2408456 | tf_op jit(solution)/shard_map/ppermute | solution.py:21
  254.4 26.0 %collective-permute-start.3 = (bf16[4,196,512]{2,0,1:T(4,128)(2,1)}, bf16[4,196,512]{2,0,1:T(4,128)(2,1)}, u32[]{:S(2)}, u32[]{:S(2)}) collective-permute-start(bf16[4,196,512]{2,0,1:T(4,128)(2,1)} %get-tuple-element.21), channel_id=1, source_target_pairs={{1,0},{2,1},{3,2},{4,3},{5,4},{6,5},{7,6},{0,7},{9,8},{10,9},{11,1... | collective-permute-start | bytes 2408456 | tf_op jit(solution)/shard_map/ppermute | solution.py:24
  307.5 61.4 %reduce-scatter.9.cloned.1.call-start = ((), (), s32[]{:S(2)}) async-start(), calls=%async_computation.3 | async-start | bytes 737280
  315.4 218.4 %all-reduce.15.cloned.1.call-start = ((), (), s32[]{:S(2)}) async-start(), calls=%async_computation.4 | async-start | bytes 12591104
  332.0 38.6 %copy-start.47 = (f32[1024]{0:T(1024)S(1)}, f32[1024]{0:T(1024)}, u32[]{:S(2)}) copy-start(f32[1024]{0:T(1024)} %param.15) | copy-start | bytes 12292
  332.0 38.6 %copy-start.56 = (f32[80]{0:T(128)S(1)}, f32[80]{0:T(128)}, u32[]{:S(2)}) copy-start(f32[80]{0:T(128)} %copy-done.55) | copy-start | bytes 964
  332.0 38.6 %copy-start.62 = (f32[80]{0:T(128)S(1)}, f32[80]{0:T(128)}, u32[]{:S(2)}) copy-start(f32[80]{0:T(128)} %copy-done.61) | copy-start | bytes 964
  376.4 6.9 %copy-start.76 = (f32[80]{0:T(128)S(1)}, f32[80]{0:T(128)}, u32[]{:S(2)}) copy-start(f32[80]{0:T(128)} %copy-done.75) | copy-start | bytes 964
  396.7 202.3 %all-reduce.17.cloned.1.call-start = ((), (), s32[]{:S(2)}) async-start(), calls=%async_computation.5 | async-start | bytes 3149824
  (65 other events, 152.3 us)
Sparse Core Ops, SparseCore 0:
  307.6 29.4 reduce-scatter.6
  339.4 29.4 reduce-scatter.8
  396.8 137.0 all-reduce.14
  537.4 61.4 all-reduce.16
where the time goes:
time: 618 us; the launch traced here: 608 us
  waiting for transfers between devices  228 us (37%)
  local copies, waits for them, and re-layouts  200 us (32%)
  matrix products  55.5 us (9%)
  blocking collectives  50.9 us (8%)
  other arithmetic  44.7 us (7%)
  between operations  20.5 us (3%)
  starting transfers between devices  7.5 us (1%)
    unnamed x8, waiting for transfers between devices  228 us
    unnamed x181, local copies, waits for them, and re-layouts  34.5 us
    all_gather x1, blocking collectives, body(): lax.all_gather(key_own, 'ctx', axis=0, tiled=True)  17.9 us
    dynamic_update_slice x1, local copies, waits for them, and re-layouts, dec_mix(): pair_win = lax.dynamic_slice_in_dim(pair_ext, slice_start, window_span, 0)  17.6 us
    unnamed x1, blocking collectives  16.8 us
    all_gather x1, blocking collectives, body(): lax.all_gather(value_own, 'ctx', axis=0, tiled=True)  16.2 us
    dot_general x3, matrix products, dec_mix(): jnp.einsum('nhqk,nhkd->nhqd', weights, value_heads, preferred_element_typ...  13.3 us
    reshape x2, local copies, waits for them, and re-layouts, dec_mix(): windows.transpose(0, 2, 4, 1, 3, 5, 6)  12.7 us
  transfers between devices with their start and end apart: 8, of which 4 were waited for; matrix products, arithmetic and copies ran while one was open for 15% of the time, Pallas kernels for 0%

commit v1 on v0

--- a/solution.py
+++ b/solution.py
@@ -1,6 +1,10 @@
+import functools
+
 import jax
 import jax.numpy as jnp
 from jax import lax
+from jax.experimental import pallas as pl
+from jax.experimental.pallas import tpu as pltpu
 from jax.sharding import PartitionSpec as P
 
 HEAD = 64
@@ -147,7 +151,7 @@
     return joined
 
 
-def body(
+def plain_body(
     patches,
     vis_index,
     shifts,
@@ -234,6 +238,701 @@
     return (d_patches, summed)
 
 
+LANES = 128
+CELLS = GRID * GRID
+WINDOW = WT * SW * SW
+SIDES = GRID // SW
+SPOTS = SIDES * SIDES
+PAD = 16
+FUSED_SLOTS = 640
+NEG = -1e30
+F32 = jnp.float32
+BF16 = jnp.bfloat16
+
+
+def mm(left, right):
+    return lax.dot_general(left, right, (((1,), (0,)), ((), ())), preferred_element_type=F32)
+
+
+def mm_nt(left, right):
+    return lax.dot_general(left, right, (((1,), (1,)), ((), ())), preferred_element_type=F32)
+
+
+def mm_tn(left, right):
+    return lax.dot_general(left, right, (((0,), (0,)), ((), ())), preferred_element_type=F32)
+
+
+def normed_rows(values):
+    center = values - jnp.mean(values, axis=-1, keepdims=True)
+    scale = lax.rsqrt(jnp.mean(center * center, axis=-1, keepdims=True) + norm_eps)
+    return center * scale, scale
+
+
+def norm_back(d_normed, unit, scale, gain):
+    d_unit = d_normed * gain
+    return scale * (
+        d_unit
+        - jnp.mean(d_unit, axis=-1, keepdims=True)
+        - unit * jnp.mean(d_unit * unit, axis=-1, keepdims=True)
+    )
+
+
+def lane_mask(head, rows, lanes):
+    lane = lax.broadcasted_iota(jnp.int32, (rows, lanes), 1)
+    return (lane >= head * HEAD) & (lane < (head + 1) * HEAD)
+
+
+def pack_kernel(shifts, tokens, slots, cot, out):
+    rows, width = cot.shape
+    front = tokens.shape[1]
+    count = slots.shape[1]
+    tok = lax.broadcasted_iota(jnp.int32, (rows, LANES), 0)
+    lane = lax.broadcasted_iota(jnp.int32, (rows, LANES), 1)
+    tok_f = tok.astype(F32)
+    step = jnp.floor((tok_f + 0.5) * (1.0 / CELLS))
+    cell = tok_f - step * CELLS
+    row = jnp.floor((cell + 0.5) * (1.0 / GRID))
+    col = cell - row * GRID
+    step_at, row_at, col_at = (shifts[0, axis].astype(F32) for axis in range(3))
+    row = row - row_at
+    row = jnp.where(row < 0, row + GRID, row)
+    col = col - col_at
+    col = jnp.where(col < 0, col + GRID, col)
+    code = jnp.where(row >= SW, float(SIDES), 0.0) + jnp.where(col >= SW, 1.0, 0.0)
+    code = code + jnp.where(step >= step_at, float(SPOTS), 0.0)
+    hits = (lax.broadcasted_iota(jnp.int32, (rows, count), 0) == slots[...]).astype(F32)
+    covered = jnp.sum(hits, axis=1, keepdims=True)
+    hits = hits.astype(BF16)
+    masked = jnp.where((lane.astype(F32) == code) & (covered < 0.5), 1.0, 0.0).astype(BF16)
+    about = jnp.where(lane == 0, code + 1.0, 0.0).astype(BF16)
+    out[:, :front] = tokens[...]
+    out[:, front : front + width] = mm_tn(hits, cot[...]).astype(BF16)
+    sums = mm_tn(masked, cot[...])[: 2 * SPOTS]
+    codes = mm_tn(about, hits)[:8]
+    codes = jnp.concatenate([codes, jnp.zeros((8, LANES - count), F32)], 1)
+    rest = [sums[:, at * LANES : (at + 1) * LANES] for at in range(width // LANES)] + [codes]
+    spare = count - 8 * len(rest)
+    rest = jnp.concatenate(rest + [jnp.zeros((spare, LANES), F32)], 0)
+    out[:, front + width :] = rest.astype(BF16)
+
+
+def flat_rows(widths):
+    places, at = [], 0
+    for rows, lanes in widths:
+        places.append(at)
+        at += rows * lanes // LANES
+    return places, at
+
+
+def store_flat(flat, widths, offset, which, lane_at, grad):
+    places, _ = flat_rows(widths)
+    stride = widths[which][1] // LANES
+    for at in range(grad.shape[1] // LANES):
+        tile = grad[:, at * LANES : (at + 1) * LANES]
+        start = places[which] - offset + lane_at // LANES + at
+        if grad.shape[0] == 1:
+            flat[start : start + 1, :] = tile
+        else:
+            flat[pl.ds(start, grad.shape[0], stride=stride), :] = tile
+
+
+def head_lanes(head, rows, lanes):
+    lane = lax.broadcasted_iota(jnp.int32, (rows, lanes), 1)
+    return (lane >= head * HEAD) & (lane < (head + 1) * HEAD)
+
+
+def clip_kernel(n_dp, n_ctx, n_blocks, widths, *refs):
+    where_at = refs[0]
+    blocks = refs[1 : 1 + n_blocks]
+    enc_gain, mask_token, dec_gain = refs[1 + n_blocks : 4 + n_blocks]
+    far = refs[4 + n_blocks : 9 + n_blocks]
+    outs = refs[9 + n_blocks :]
+    d_patches = outs[0]
+    pieces = outs[1 : 1 + n_dp]
+    (
+        nrm,
+        nrm_t,
+        qkv,
+        weights,
+        mixed,
+        res,
+        dec_in,
+        dec_proj,
+        hot,
+        sums,
+        d_mixes,
+        d_acc,
+        blk_mix,
+        blk_cot,
+        wide,
+        q_stack,
+        d_stack,
+        p_stack,
+        d_p_stack,
+        d_query,
+        d_keys,
+        d_values,
+        d_latent,
+        d_mixed,
+        turned,
+        d_scores,
+        d_kv_t,
+        d_qkv,
+        bias,
+        enc_qkv_here,
+        enc_out_here,
+        enc_to_dec_here,
+        dec_qkv_here,
+        dec_out_here,
+        flat,
+        cut,
+        sems,
+    ) = outs[1 + n_dp :]
+    here = (enc_qkv_here, enc_out_here, enc_to_dec_here, dec_qkv_here, dec_out_here)
+    loads = [
+        pltpu.make_async_copy(far[at], here[at], sems.at[at]) for at in range(len(here))
+    ]
+    loads[0].start()
+    core = where_at[0]
+    count, width = blocks[0].shape[0], enc_gain.shape[1]
+    slots = n_ctx * count
+    chans = enc_out_here.shape[0]
+    dec_chans, dec_width = dec_out_here.shape
+    group_lanes = 4 * HEAD
+    groups = chans // group_lanes
+    scale = HEAD ** (-0.5)
+    half = n_ctx // 2
+    spread = 2 * SPOTS
+    size = count + PAD
+    chunk = slots // 2
+
+    tokens_at = slice(0, width)
+    cots_at = slice(width, width + dec_width)
+    rest_at = slice(width + dec_width, width + dec_width + LANES)
+
+    def pick(at, lanes):
+        chip = where_at[2] // 2
+        block = blocks[at][:, lanes]
+        hop = at % half
+        if n_blocks == n_ctx or hop not in (1, half - 1):
+            return block
+        other = blocks[n_ctx + at // half][:, lanes]
+        return jnp.where(chip == (half - 1 if hop == 1 else 0), other, block)
+
+    def codes_of(rest):
+        at = spread * dec_width // LANES
+        return rest[at : at + 8, :count]
+
+    for at in range(n_ctx):
+        rows = slice(at * count, (at + 1) * count)
+        unit, _ = normed_rows(pick(at, tokens_at).astype(F32))
+        nrm[rows, :] = (unit * enc_gain[...]).astype(BF16)
+        codes = codes_of(pick(at, rest_at).astype(F32))[:1]
+        bias[:, rows] = jnp.broadcast_to(jnp.where(codes > 0.5, 0.0, NEG), (8, count))
+    for load in loads[1:]:
+        load.start()
+    loads[0].wait()
+
+    for at in range(3 * groups):
+        lanes = slice(at * group_lanes, (at + 1) * group_lanes)
+        qkv[:, lanes] = mm(nrm[...], enc_qkv_here[:, lanes]).astype(BF16)
+    nrm_t[...] = nrm[...].T
+
+    def lanes_of(group):
+        return [
+            pl.ds(pl.multiple_of(at * chans + group * group_lanes, group_lanes), group_lanes)
+            for at in range(3)
+        ]
+
+    def attend(group, carry):
+        lanes, key_lanes, value_lanes = lanes_of(group)
+        keys = qkv[:, key_lanes]
+        values = qkv[:, value_lanes]
+        for head in range(4):
+            own = head_lanes(head, chunk, group_lanes)
+            for part in range(slots // chunk):
+                rows = slice(part * chunk, (part + 1) * chunk)
+                query = jnp.where(own, qkv[rows, lanes].astype(F32) * scale, 0.0).astype(BF16)
+                scores = mm_nt(query, keys) + bias[:1]
+                raised = jnp.exp(scores - jnp.max(scores, axis=-1, keepdims=True))
+                share = (raised * (1.0 / jnp.sum(raised, axis=-1, keepdims=True))).astype(BF16)
+                weights[group * 4 + head, rows, :] = share
+                mix = mm(share, values)
+                if head > 0:
+                    mix = jnp.where(own, mix, mixed[rows, lanes].astype(F32))
+                mixed[rows, lanes] = mix.astype(BF16)
+        return carry
+
+    lax.fori_loop(0, groups, attend, 0)
+
+    loads[1].wait()
+    loads[2].wait()
+    for at in range(n_ctx):
+        rows = slice(at * count, (at + 1) * count)
+        out = pick(at, tokens_at).astype(F32) + mm(mixed[rows, :], enc_out_here[...])
+        res[rows, :] = out.astype(BF16)
+    latent = mm(res[...], enc_to_dec_here[...]).astype(BF16)
+    d_latent[...] = latent
+
+    def place(shard, on_core):
+        at = shard // 2
+        if shard % 2 == 0:
+            return at
+        return half + (at + on_core) % half
+
+    def rows_of(shard):
+        shard = shard % n_ctx
+        return slice(shard * count, (shard + 1) * count)
+
+    lane = lax.broadcasted_iota(jnp.int32, (count, LANES), 1).astype(F32)
+    square = [lax.broadcasted_iota(jnp.int32, (count, count), axis) for axis in range(2)]
+    unity = jnp.where(square[0] == square[1], 1.0, 0.0).astype(BF16)
+
+    def in_time(shard, at):
+        dec_in[rows_of(shard), :] = d_latent[rows_of(at), :]
+        blk_cot[shard * size : shard * size + count, :] = pick(at, cots_at)
+        rest = pick(at, rest_at).astype(F32)
+        sums[shard * spread : (shard + 1) * spread, :] = jnp.concatenate(
+            [rest[tile * spread : (tile + 1) * spread] for tile in range(dec_width // LANES)], 1
+        )
+        code = mm_nt(unity, codes_of(rest).astype(BF16))[:, :1] - 1.0
+        last = (shard + n_ctx - 1) % n_ctx
+        window = code + jnp.where(
+            code >= SPOTS, float((shard - 1) * SPOTS), float(last * SPOTS)
+        )
+        hit = (lane == window) & (code >= 0.0)
+        hot[rows_of(shard), :] = jnp.where(hit, 1.0, 0.0).astype(BF16)
+
+    for shard in range(0, n_ctx, 2):
+        in_time(shard, place(shard, 0))
+    for on_core in range(2):
+
+        @pl.when(core == on_core)
+        def _():
+            for shard in range(1, n_ctx, 2):
+                in_time(shard, place(shard, on_core))
+
+    loads[3].wait()
+    loads[4].wait()
+    dec_in[slots:, :] = jnp.broadcast_to(mask_token[...], (PAD, dec_width)).astype(BF16)
+    for shard in range(n_ctx):
+        after = (shard + 1) % n_ctx
+        rows_sum = (
+            sums[shard * spread + SPOTS : (shard + 1) * spread, :]
+            + sums[after * spread : after * spread + SPOTS, :]
+        )
+        blk_cot[shard * size + count : (shard + 1) * size, :] = jnp.concatenate(
+            [rows_sum, jnp.zeros((PAD - SPOTS, dec_width), F32)], 0
+        ).astype(BF16)
+
+    dec_unit, dec_scale = normed_rows(dec_in[...].astype(F32))
+    dec_nrm = (dec_unit * dec_gain[...]).astype(BF16)
+    dec_proj[...] = mm(dec_nrm, dec_qkv_here[...]).astype(BF16)
+    d_mixes[...] = mm_nt(blk_cot[...], dec_out_here[...]).astype(BF16)
+
+    pad_row = lax.broadcasted_iota(jnp.int32, (PAD, LANES), 0)
+    pad_lane = lax.broadcasted_iota(jnp.int32, (PAD, LANES), 1)
+    reach = 3 * count + PAD
+    col = lax.broadcasted_iota(jnp.int32, (size, reach), 1)
+    owns = [head_lanes(head, size, dec_chans) for head in range(dec_chans // HEAD)]
+    tall = len(owns) * size
+    mask_rows = slice(slots, slots + PAD)
+    query_lanes = slice(0, dec_chans)
+    key_lanes = slice(dec_chans, 2 * dec_chans)
+    value_lanes = slice(2 * dec_chans, 3 * dec_chans)
+
+    def stack_heads(rows):
+        return jnp.concatenate([jnp.where(own, rows, 0.0) for own in owns], 0)
+
+    def unstack_heads(rows):
+        total = jnp.where(owns[0], rows[:size], 0.0)
+        for head in range(1, len(owns)):
+            total = jnp.where(owns[head], rows[head * size : (head + 1) * size], total)
+        return total
+
+    def rows_at(shard, rows):
+        return pl.ds(pl.multiple_of(shard * rows, PAD), rows)
+
+    def near(ref, shard, lanes, last):
+        shards = [lax.rem(shard + n_ctx + step, n_ctx) for step in (-1, 0, 1)]
+        return jnp.concatenate([ref[rows_at(at, count), lanes] for at in shards] + [last], 0)
+
+    def keys_of(shard):
+        return near(dec_proj, shard, key_lanes, dec_proj[mask_rows, key_lanes])
+
+    def values_of(shard):
+        return near(dec_proj, shard, value_lanes, dec_proj[mask_rows, value_lanes])
+
+    def score(shard, here):
+        eye = (pad_row + shard * SPOTS == pad_lane) & (pad_row < SPOTS)
+        eye = jnp.where(eye, 1.0, 0.0).astype(BF16)
+        hot_keys = near(hot, shard, slice(None), jnp.zeros((PAD, LANES), BF16))
+        match = mm_nt(jnp.concatenate([hot[rows_at(shard, count), :], eye], 0), hot_keys)
+        masked = float(WINDOW) - jnp.sum(match, axis=1, keepdims=True)
+        mask_bias = jnp.where(masked > 0.5, jnp.log(jnp.maximum(masked, 1.0)), NEG)
+        block_bias = jnp.where(match > 0.5, 0.0, jnp.where(col == 3 * count, mask_bias, NEG))
+        queries = jnp.concatenate(
+            [dec_proj[rows_at(shard, count), query_lanes], dec_proj[mask_rows, query_lanes]], 0
+        )
+        queries = stack_heads(queries.astype(F32) * scale).astype(BF16)
+        q_stack[here, :] = queries
+        d_stack[here, :] = stack_heads(d_mixes[rows_at(shard, size), :].astype(F32)).astype(BF16)
+        wide[here, :] = mm_nt(queries, keys_of(shard)) + jnp.concatenate(
+            [block_bias] * len(owns), 0
+        )
+
+    def soften():
+        scores = wide[...]
+        raised = jnp.exp(scores - jnp.max(scores, axis=-1, keepdims=True))
+        share = raised * (1.0 / jnp.sum(raised, axis=-1, keepdims=True))
+        p_stack[...] = share.astype(BF16)
+
+    def mix(shard, here):
+        values = values_of(shard)
+        blk_mix[rows_at(shard, size), :] = unstack_heads(mm(p_stack[here, :], values)).astype(BF16)
+        wide[here, :] = mm_nt(d_stack[here, :], values)
+
+    def soften_back():
+        share = p_stack[...].astype(F32)
+        d_share = wide[...]
+        delta = jnp.sum(d_share * share, axis=-1, keepdims=True)
+        d_p_stack[...] = (share * (d_share - delta)).astype(BF16)
+
+    def mix_back(shard, here):
+        d_score = d_p_stack[here, :]
+        d_query[rows_at(shard, size), :] = unstack_heads(mm(d_score, keys_of(shard))) * scale
+        d_keys[shard] = mm_tn(d_score, q_stack[here, :]).astype(BF16)
+        d_values[shard] = mm_tn(p_stack[here, :], d_stack[here, :]).astype(BF16)
+
+    def two_shards(at, carry):
+        both = [(2 * at + one, slice(one * tall, (one + 1) * tall)) for one in range(2)]
+        for shard, here in both:
+            score(shard, here)
+        soften()
+        for shard, here in both:
+            mix(shard, here)
+        soften_back()
+        for shard, here in both:
+            mix_back(shard, here)
+        return carry
+
+    lax.fori_loop(0, half, two_shards, 0)
+
+    mask_d_query = jnp.zeros((1, dec_chans), F32)
+    mask_d_pair = [jnp.zeros((1, dec_chans), F32) for _ in range(2)]
+    for shard in range(n_ctx):
+        rows = rows_of(shard)
+        d_acc[rows, query_lanes] = d_query[shard * size : shard * size + count, :].astype(BF16)
+        mask_d_query += jnp.sum(
+            d_query[shard * size + count : shard * size + count + SPOTS, :], 0, keepdims=True
+        )
+        for at, (lanes, ref) in enumerate(((key_lanes, d_keys), (value_lanes, d_values))):
+            before, after = (shard + n_ctx - 1) % n_ctx, (shard + 1) % n_ctx
+            total = (
+                ref[before, 2 * count : 3 * count, :].astype(F32)
+                + ref[shard, count : 2 * count, :].astype(F32)
+                + ref[after, :count, :].astype(F32)
+            )
+            d_acc[rows, lanes] = total.astype(BF16)
+            mask_d_pair[at] += ref[shard, 3 * count :, :].astype(F32)[:1]
+    first = lax.broadcasted_iota(jnp.int32, (PAD, 3 * dec_chans), 0) == 0
+    mask_d = jnp.concatenate([mask_d_query] + mask_d_pair, 1)
+    d_acc[mask_rows, :] = jnp.where(first, mask_d, 0.0).astype(BF16)
+
+    d_dec_proj = d_acc[...]
+    d_dec_nrm = mm_nt(d_dec_proj, dec_qkv_here[...])
+    g_dec_qkv = mm_tn(dec_nrm, d_dec_proj)
+    g_dec_out = mm_tn(blk_mix[...], blk_cot[...])
+    g_dec_gain = jnp.sum(d_dec_nrm * dec_unit, axis=0, keepdims=True)
+    d_dec_in = norm_back(d_dec_nrm, dec_unit, dec_scale, dec_gain[...])
+    g_mask = jnp.sum(sums[...], axis=0, keepdims=True) + d_dec_in[slots : slots + 1]
+    for shard in range(n_ctx):
+        cot = blk_cot[shard * size : shard * size + count, :].astype(F32)
+        back = d_dec_in[shard * count : (shard + 1) * count].astype(BF16).astype(F32)
+        dec_in[rows_of(shard), :] = (cot + back).astype(BF16)
+    for on_core in range(2):
+
+        @pl.when(core == on_core)
+        def _():
+            for shard in range(n_ctx):
+                d_latent[rows_of(place(shard, on_core)), :] = dec_in[rows_of(shard), :]
+
+    d_res = nrm
+    d_res[...] = mm_nt(d_latent[...], enc_to_dec_here[...]).astype(BF16)
+    d_mixed[...] = mm_nt(d_res[...], enc_out_here[...]).astype(BF16)
+
+    def store(which, lane_at, grad):
+        store_flat(flat, widths, 0, which, lane_at, grad)
+
+    store(2, 0, mm_tn(mixed[...], d_res[...]))
+    store(3, 0, mm_tn(res[...], d_latent[...]))
+    store(4, 0, g_mask)
+    store(5, 0, g_dec_gain)
+    store(6, 0, g_dec_qkv)
+    store(7, 0, g_dec_out)
+
+    def attend_back(group, carry):
+        lanes, key_lanes, value_lanes = lanes_of(group)
+        turned[:group_lanes, :] = qkv[:, lanes].T
+        turned[group_lanes:, :] = d_mixed[:, lanes].T
+        keys = qkv[:, key_lanes]
+        values = qkv[:, value_lanes]
+        for head in range(4):
+            own = head_lanes(head, chunk, group_lanes)
+            at_head = group * 4 + head
+            for part in range(slots // chunk):
+                rows = slice(part * chunk, (part + 1) * chunk)
+                cot = jnp.where(own, d_mixed[rows, lanes].astype(F32), 0.0)
+                delta = jnp.sum(cot * mixed[rows, lanes].astype(F32), axis=-1, keepdims=True)
+                d_share = mm_nt(cot.astype(BF16), values)
+                d_score = weights[at_head, rows, :].astype(F32) * (d_share - delta)
+                d_score = d_score.astype(BF16)
+                d_scores[head % 2, rows, :] = d_score
+                d_query = mm(d_score, keys) * scale
+                if head > 0:
+                    d_query = jnp.where(own, d_query, d_qkv[rows, lanes].astype(F32))
+                d_qkv[rows, lanes] = d_query.astype(BF16)
+            to_key = pl.ds(pl.multiple_of(at_head * HEAD, HEAD), HEAD)
+            to_value = pl.ds(pl.multiple_of(chans + at_head * HEAD, HEAD), HEAD)
+            query_t = turned[head * HEAD : (head + 1) * HEAD, :]
+            cot_t = turned[group_lanes + head * HEAD : group_lanes + (head + 1) * HEAD, :]
+            d_kv_t[to_key, :] = mm(query_t, d_scores[head % 2]) * scale
+            d_kv_t[to_value, :] = mm(cot_t, weights[at_head])
+        return carry
+
+    lax.fori_loop(0, groups, attend_back, 0)
+    d_qkv[:, chans:] = d_kv_t[...].T.astype(BF16)
+
+    places, total = flat_rows(widths)
+    gain_sum = jnp.zeros((width, LANES), F32)
+    for at in range(3 * groups):
+        lanes = slice(at * group_lanes, (at + 1) * group_lanes)
+        grad = mm(nrm_t[...], d_qkv[:, lanes])
+        store(1, at * group_lanes, grad)
+        weighed = grad * enc_qkv_here[:, lanes].astype(F32)
+        for to in range(group_lanes // LANES):
+            gain_sum += weighed[:, to * LANES : (to + 1) * LANES]
+    store(0, 0, jnp.sum(gain_sum.T, axis=0, keepdims=True) / enc_gain[...])
+    d_own = mm_nt(d_qkv[:count, :], enc_qkv_here[...])
+    unit, unit_scale = normed_rows(blocks[0][:, tokens_at].astype(F32))
+    d_own = norm_back(d_own, unit, unit_scale, enc_gain[...]).astype(BF16).astype(F32)
+    d_patches[...] = (d_res[:count, :].astype(F32) + d_own).astype(BF16)
+
+    piece_rows = cut.shape[1]
+    half_rows = 2 * total // (n_dp * n_ctx)
+
+    def cut_piece(to, carry):
+        start = (to * n_ctx + where_at[2]) * half_rows // 2
+        slot = lax.rem(to - where_at[1] + n_dp, n_dp)
+        shift = lax.rem(start, 8)
+        base = start - shift
+        for small in range(8):
+
+            @pl.when(shift == small)
+            def _():
+                rows = flat[pl.ds(pl.multiple_of(base, 8), piece_rows + 8), :]
+                cut[slot] = rows[small : small + piece_rows].astype(BF16)
+
+        return carry
+
+    lax.fori_loop(0, n_dp, cut_piece, 0)
+    for at in range(n_dp):
+        pieces[at][...] = cut[at]
+
+
+def join_kernel(where_at, *refs):
+    out = refs[-1]
+    total = refs[0][...].astype(F32)
+    for ref in refs[1:-1]:
+        total = total + ref[...].astype(F32)
+    rows = out.shape[0]
+    odd = lax.rem(where_at[2], 2) == 1
+
+    @pl.when(odd)
+    def _():
+        turned = pltpu.roll(total, LANES // 2, 1)
+        lane = lax.broadcasted_iota(jnp.int32, (rows, LANES), 1)
+        out[...] = jnp.where(lane < LANES // 2, turned, pltpu.roll(turned, rows - 1, 0))
+
+    @pl.when(jnp.logical_not(odd))
+    def _():
+        out[...] = total
+
+
+def fused_body(
+    n_dp,
+    n_ctx,
+    patches,
+    vis_index,
+    shifts,
+    enc_gain,
+    enc_qkv,
+    enc_out,
+    enc_to_dec,
+    mask_token,
+    dec_gain,
+    dec_qkv,
+    dec_out,
+    dec_cot,
+):
+    tokens = patches[0]
+    params = (enc_gain, enc_qkv, enc_out, enc_to_dec, mask_token, dec_gain, dec_qkv, dec_out)
+    widths = [(1,) * (2 - param.ndim) + param.shape for param in params]
+    half = n_ctx // 2
+
+    def by_hops(block):
+        def shift(array, hops, chips):
+            pairs = [((chip + hops) % half, chip) for chip in chips]
+            turn = [(2 * pair[0] + core, 2 * pair[1] + core) for pair in pairs for core in range(2)]
+            return lax.ppermute(array, "ctx", turn)
+
+        def swap(array, chips):
+            return lax.ppermute(
+                array, "ctx", [(2 * chip + core, 2 * chip + 1 - core) for chip in chips for core in range(2)]
+            )
+
+        every = range(half)
+        if half != 4:
+            near = [block] + [shift(block, step, every) for step in range(1, half)]
+            return near + [swap(other, every) for other in near]
+        where = (every, every[:-1], every, every[1:], (0, half - 1))
+        middle = shift(block, 2, every)
+        first, last = shift(block, 1, where[1]), shift(block, 3, where[3])
+        ends = lax.ppermute(
+            middle, "ctx", [(2 * a + core, 2 * b + core) for a, b in ((1, 0), (2, 3)) for core in range(2)]
+        )
+        near = [block, first, middle, last, ends]
+        far = [swap(other, chips) for other, chips in zip(near, where)]
+        return near[:4] + far[:4] + [near[4], far[4]]
+
+    blocks = by_hops(call_pack(shifts, tokens, vis_index, dec_cot[0]))
+    dp_at, ctx_at = lax.axis_index("dp"), lax.axis_index("ctx")
+    where_at = jnp.stack([ctx_at % 2, dp_at, ctx_at]).astype(jnp.int32)
+    d_patches, *pieces = call_clip(n_dp, n_ctx, widths, where_at, blocks, params)
+    got = [pieces[0]]
+    for step in range(1, n_dp):
+        turn = [(at, (at + step) % n_dp) for at in range(n_dp)]
+        got.append(lax.ppermute(pieces[step], "dp", turn))
+    share = flat_rows(widths)[1] * LANES // (n_dp * n_ctx)
+    return d_patches[None], call_join(where_at, got).reshape(-1)[:share]
+
+
+def piece_shape(n_dp, n_ctx, widths):
+    share = flat_rows(widths)[1] * LANES // (n_dp * n_ctx)
+    rows = -(-(share + LANES // 2) // LANES)
+    return jax.ShapeDtypeStruct((-(-rows // PAD) * PAD, LANES), BF16)
+
+
+IN_VMEM = pl.BlockSpec(memory_space=pltpu.VMEM)
+IN_SMEM = pl.BlockSpec(memory_space=pltpu.SMEM)
+ANYWHERE = pl.BlockSpec(memory_space=pl.ANY)
+
+
+def call_pack(shifts, tokens, vis_index, cot):
+    count, width = tokens.shape
+    return pl.pallas_call(
+        pack_kernel,
+        out_shape=jax.ShapeDtypeStruct((count, width + cot.shape[1] + LANES), BF16),
+        in_specs=[IN_SMEM, IN_VMEM, IN_VMEM, IN_VMEM],
+        out_specs=IN_VMEM,
+        name="pack",
+    )(shifts, tokens, vis_index, cot)
+
+
+def call_clip(n_dp, n_ctx, widths, where_at, blocks, params):
+    enc_gain, enc_qkv, enc_out, enc_to_dec, mask_token, dec_gain, dec_qkv, dec_out = params
+    count, width = blocks[0].shape[0], enc_gain.shape[0]
+    slots = n_ctx * count
+    chans = enc_out.shape[0]
+    dec_chans, dec_width = dec_out.shape
+    total = flat_rows(widths)[1]
+    piece = piece_shape(n_dp, n_ctx, widths)
+    size = count + PAD
+    tall = dec_chans // HEAD * size
+    reach = 3 * count + PAD
+    matrices = (enc_qkv, enc_out, enc_to_dec, dec_qkv, dec_out)
+    return pl.pallas_call(
+        functools.partial(clip_kernel, n_dp, n_ctx, len(blocks), widths),
+        out_shape=[jax.ShapeDtypeStruct((count, width), BF16)] + [piece] * n_dp,
+        in_specs=[IN_SMEM] + [IN_VMEM] * (len(blocks) + 3) + [ANYWHERE] * len(matrices),
+        out_specs=[IN_VMEM] * (1 + n_dp),
+        scratch_shapes=[
+            pltpu.VMEM((slots, width), BF16),
+            pltpu.VMEM((width, slots), BF16),
+            pltpu.VMEM((slots, 3 * chans), BF16),
+            pltpu.VMEM((chans // HEAD, slots, slots), BF16),
+            pltpu.VMEM((slots, chans), BF16),
+            pltpu.VMEM((slots, width), BF16),
+            pltpu.VMEM((slots + PAD, dec_width), BF16),
+            pltpu.VMEM((slots + PAD, 3 * dec_chans), BF16),
+            pltpu.VMEM((slots, LANES), BF16),
+            pltpu.VMEM((n_ctx * 2 * SPOTS, dec_width), F32),
+            pltpu.VMEM((n_ctx * size, dec_chans), BF16),
+            pltpu.VMEM((slots + PAD, 3 * dec_chans), BF16),
+            pltpu.VMEM((n_ctx * size, dec_chans), BF16),
+            pltpu.VMEM((n_ctx * size, dec_width), BF16),
+            pltpu.VMEM((2 * tall, reach), F32),
+            pltpu.VMEM((2 * tall, dec_chans), BF16),
+            pltpu.VMEM((2 * tall, dec_chans), BF16),
+            pltpu.VMEM((2 * tall, reach), BF16),
+            pltpu.VMEM((2 * tall, reach), BF16),
+            pltpu.VMEM((n_ctx * size, dec_chans), F32),
+            pltpu.VMEM((n_ctx, reach, dec_chans), BF16),
+            pltpu.VMEM((n_ctx, reach, dec_chans), BF16),
+            pltpu.VMEM((slots, dec_width), BF16),
+            pltpu.VMEM((slots, chans), BF16),
+            pltpu.VMEM((8 * HEAD, slots), BF16),
+            pltpu.VMEM((2, slots, slots), BF16),
+            pltpu.VMEM((2 * chans, slots), F32),
+            pltpu.VMEM((slots, 3 * chans), BF16),
+            pltpu.VMEM((8, slots), F32),
+        ]
+        + [pltpu.VMEM(matrix.shape, BF16) for matrix in matrices]
+        + [
+            pltpu.VMEM((total + 2 * PAD, LANES), F32),
+            pltpu.VMEM((n_dp,) + piece.shape, BF16),
+            pltpu.SemaphoreType.DMA((len(matrices),)),
+        ],
+        compiler_params=pltpu.CompilerParams(vmem_limit_bytes=VMEM_BYTES),
+        cost_estimate=pl.CostEstimate(
+            flops=40 * 10**9, bytes_accessed=16 * 2**20, transcendentals=0
+        ),
+        name="clip",
+    )(
+        where_at,
+        *blocks,
+        enc_gain[None],
+        mask_token[None],
+        dec_gain[None],
+        *matrices,
+    )
+
+
+def call_join(where_at, blocks):
+    return pl.pallas_call(
+        join_kernel,
+        out_shape=jax.ShapeDtypeStruct(blocks[0].shape, F32),
+        in_specs=[IN_SMEM] + [IN_VMEM] * len(blocks),
+        out_specs=IN_VMEM,
+        name="join",
+    )(where_at, *blocks)
+
+
+VMEM_BYTES = 56 * 1024 * 1024
+
+
+def body(n_dp, n_ctx, patches, vis_index, *rest):
+    enc_qkv = rest[2]
+    dec_cot = rest[-1]
+    head = enc_qkv.shape[0] * (1 + enc_qkv.shape[1])
+    length = sum(param.size for param in rest[1:-1])
+    small = n_ctx * patches.shape[1] <= FUSED_SLOTS
+    whole = head * n_dp % length == 0 and dec_cot.shape[1] == WT * CELLS
+    if small and n_ctx % 2 == 0 and whole:
+        return fused_body(n_dp, n_ctx, patches, vis_index, *rest)
+    return plain_body(patches, vis_index, *rest)
+
+
 def solution(mesh):
     in_specs = (
         P("dp", "ctx", None),
@@ -250,4 +949,4 @@
         P("dp", "ctx", None),
     )
     out_specs = (P("dp", "ctx", None), P(("dp", "ctx")))
-    return jax.shard_map(body, mesh=mesh, in_specs=in_specs, out_specs=out_specs, check_vma=False)
+    return jax.shard_map(functools.partial(body, mesh.shape["dp"], mesh.shape["ctx"]), mesh=mesh, in_specs=in_specs, out_specs=out_specs, check_vma=False)

time: 618 us -> 93.3 us (0.15); the launches traced: 608 us -> 92.9 us
  waiting for transfers between devices: 228 us -> 23.1 us
  local copies, waits for them, and re-layouts: 200 us -> 3.13 us
  matrix products: 55.5 us -> 0 us
  blocking collectives: 50.9 us -> 0 us
  Pallas kernels: 0 us -> 45.6 us
  other arithmetic: 44.7 us -> 0.56 us
  between operations: 20.5 us -> 0.81 us
  starting transfers between devices: 7.5 us -> 19.7 us
    unnamed x8 -> x0, waiting for transfers between devices: 228 us -> none
    reshape x23 -> x0, local copies, waits for them, and re-layouts: 70.6 us -> none  [the longest x2 12.7 us: dec_mix(): windows.transpose(0, 2, 4, 1, 3, 5, 6)]
    dot_general x26 -> x0, matrix products: 55.5 us -> none  [the longest x3 13.3 us: dec_mix(): jnp.einsum('nhqk,nhkd->nhqd', weights, value_heads, preferred_element_typ...]
    pallas_call x0 -> x3, Pallas kernels: none -> 45.6 us  [the longest x1 40.5 us: call_clip(): pl.pallas_call(functools.partial(clip_kernel, n_dp, n_ctx, len(blocks), w...]
    all_gather x2 -> x0, blocking collectives: 34 us -> none  [the longest x1 17.9 us: body(): lax.all_gather(key_own, 'ctx', axis=0, tiled=True)]
    unnamed x181 -> x24, local copies, waits for them, and re-layouts: 34.5 us -> 1.36 us
    dynamic_update_slice x5 -> x0, local copies, waits for them, and re-layouts: 27.8 us -> none  [the longest x1 17.6 us: dec_mix(): pair_win = lax.dynamic_slice_in_dim(pair_ext, slice_start, window_span, 0)]
    ppermute x4 -> x12, waiting for transfers between devices: 0.01 us -> 23.1 us  [the longest x3 10.8 us: shift(): return lax.ppermute(array, 'ctx', turn)]
  transfers between devices with their start and end apart: 8 -> 12, of which waited for: 4 -> 7; matrix products, arithmetic and copies ran while one was open for 15% -> 1% of each run, Pallas kernels for 0% -> 0%
where the time goes in v1:
time: 93.3 us; the launch traced here: 92.9 us
  Pallas kernels  45.6 us (49%)
  waiting for transfers between devices  23.1 us (25%)
  starting transfers between devices  19.7 us (21%)
  local copies, waits for them, and re-layouts  3.13 us (3%)
    pallas_call x1, Pallas kernels, call_clip(): pl.pallas_call(functools.partial(clip_kernel, n_dp, n_ctx, len(blocks), w...  40.5 us
    ppermute x3, waiting for transfers between devices, shift(): return lax.ppermute(array, 'ctx', turn)  10.8 us
    ppermute x3, starting transfers between devices, shift(): return lax.ppermute(array, 'ctx', turn)  8.81 us
    ppermute x3, waiting for transfers between devices, fused_body(): got.append(lax.ppermute(pieces[step], 'dp', turn))  8.1 us
    ppermute x5, starting transfers between devices, swap(): lax.ppermute(array, 'ctx', [(2 * chip + core, 2 * chip + 1 - core) for ch...  5.05 us
    ppermute x3, starting transfers between devices, fused_body(): got.append(lax.ppermute(pieces[step], 'dp', turn))  4.55 us
    ppermute x1, waiting for transfers between devices, by_hops(): lax.ppermute(middle, 'ctx', [(2 * a + core, 2 * b + core) for a, b in ((1...  3.29 us
    pallas_call x1, Pallas kernels, call_pack(): pl.pallas_call(pack_kernel, out_shape=jax.ShapeDtypeStruct((count, width...  2.88 us
  transfers between devices with their start and end apart: 12, of which 7 were waited for; matrix products, arithmetic and copies ran while one was open for 1% of the time, Pallas kernels for 0%

profile of v1, /device:TPU:0, one launch (start us, length us, event | category | flops | bytes accessed | tf_op | source)
XLA Modules:
  0.0 92.9 jit_solution(2532646595479129628)
XLA Ops:
  0.6 2.9 %pack.1.refs_1_ = bf16[80,1664]{1,0:T(8,128)(2,1)} custom-call(s32[1,3]{1,0:T(1,128)} %shifts.1, bf16[80,1024]{1,0:T(8,128)(2,1)} %bitcast.12, s32[1,80]{1,0:T(1,128)} %slots.1, bf16[784,512]{1,0:T(8,128)(2,1)} %bitcast.11), custom_call_target="tpu_custom_call" | custom-call | tf_op jit(solution)/shard_map/pack/pallas_call | solution.py:833
  3.5 4.0 %collective-permute-start.1 = (bf16[80,1664]{1,0:T(8,128)(2,1)}, bf16[80,1664]{1,0:T(8,128)(2,1)S(1)}, u32[]{:S(2)}, u32[]{:S(2)}) collective-permute-start(bf16[80,1664]{1,0:T(8,128)(2,1)} %pack.1.refs_1_), channel_id=1, source_target_pairs={{4,0},{5,1},{6,2},{7,3},{0,4},{1,5},{2,6},{3,7},{12,8},{13,9},{14,... | collective-permute-start | bytes 798728 | tf_op jit(solution)/shard_map/ppermute | solution.py:787
  7.5 3.5 %collective-permute-start.2 = (bf16[80,1664]{1,0:T(8,128)(2,1)}, bf16[80,1664]{1,0:T(8,128)(2,1)S(1)}, u32[]{:S(2)}, u32[]{:S(2)}) collective-permute-start(bf16[80,1664]{1,0:T(8,128)(2,1)} %pack.1.refs_1_), channel_id=1, source_target_pairs={{0,2},{1,3},{2,4},{3,5},{4,6},{5,7},{8,10},{9,11},{10,12},{11,13},... | collective-permute-start | bytes 798728 | tf_op jit(solution)/shard_map/ppermute | solution.py:787
  11.0 1.3 %collective-permute-start = (bf16[80,1664]{1,0:T(8,128)(2,1)}, bf16[80,1664]{1,0:T(8,128)(2,1)S(1)}, u32[]{:S(2)}, u32[]{:S(2)}) collective-permute-start(bf16[80,1664]{1,0:T(8,128)(2,1)} %pack.1.refs_1_), channel_id=1, source_target_pairs={{2,0},{3,1},{4,2},{5,3},{6,4},{7,5},{10,8},{11,9},{12,10},{13,11},... | collective-permute-start | bytes 798728 | tf_op jit(solution)/shard_map/ppermute | solution.py:787
  12.3 8.4 %collective-permute-done.1.refs_3_ = bf16[80,1664]{1,0:T(8,128)(2,1)S(1)} collective-permute-done((bf16[80,1664]{1,0:T(8,128)(2,1)}, bf16[80,1664]{1,0:T(8,128)(2,1)S(1)}, u32[]{:S(2)}, u32[]{:S(2)}) %collective-permute-start.1) | collective-permute-done | bytes 266272 | tf_op jit(solution)/shard_map/ppermute | solution.py:787
  20.7 1.3 %collective-permute-start.7 = (bf16[80,1664]{1,0:T(8,128)(2,1)S(1)}, bf16[80,1664]{1,0:T(8,128)(2,1)S(1)}, u32[]{:S(2)}, u32[]{:S(2)}) collective-permute-start(bf16[80,1664]{1,0:T(8,128)(2,1)S(1)} %collective-permute-done.1.refs_3_), channel_id=1, source_target_pairs={{2,0},{3,1},{4,6},{5,7},{10,8},{11,9},{12,14},{13,15},{18,16},{19,... | collective-permute-start | bytes 798728 | tf_op jit(solution)/shard_map/ppermute | solution.py:801
  22.1 0.5 collective-permute-start.5
  22.6 0.7 collective-permute-start.6
  23.3 2.4 %collective-permute-done.refs_2_ = bf16[80,1664]{1,0:T(8,128)(2,1)S(1)} collective-permute-done((bf16[80,1664]{1,0:T(8,128)(2,1)}, bf16[80,1664]{1,0:T(8,128)(2,1)S(1)}, u32[]{:S(2)}, u32[]{:S(2)}) %collective-permute-start) | collective-permute-done | bytes 266272 | tf_op jit(solution)/shard_map/ppermute | solution.py:787
  25.7 1.9 %collective-permute-start.4 = (bf16[80,1664]{1,0:T(8,128)(2,1)S(1)}, bf16[80,1664]{1,0:T(8,128)(2,1)S(1)}, u32[]{:S(2)}, u32[]{:S(2)}) collective-permute-start(bf16[80,1664]{1,0:T(8,128)(2,1)S(1)} %collective-permute-done.refs_2_), channel_id=1, source_target_pairs={{0,1},{1,0},{2,3},{3,2},{4,5},{5,4},{8,9},{9,8},{10,11},{11,10},{1... | collective-permute-start | bytes 798728 | tf_op jit(solution)/shard_map/ppermute | solution.py:790
  27.6 3.3 %collective-permute-done.7.refs_9_ = bf16[80,1664]{1,0:T(8,128)(2,1)S(1)} collective-permute-done((bf16[80,1664]{1,0:T(8,128)(2,1)S(1)}, bf16[80,1664]{1,0:T(8,128)(2,1)S(1)}, u32[]{:S(2)}, u32[]{:S(2)}) %collective-permute-start.7) | collective-permute-done | bytes 266272 | tf_op jit(solution)/shard_map/ppermute | solution.py:801
  30.9 1.9 %collective-permute-start.8 = (bf16[80,1664]{1,0:T(8,128)(2,1)S(1)}, bf16[80,1664]{1,0:T(8,128)(2,1)S(1)}, u32[]{:S(2)}, u32[]{:S(2)}) collective-permute-start(bf16[80,1664]{1,0:T(8,128)(2,1)S(1)} %collective-permute-done.7.refs_9_), channel_id=1, source_target_pairs={{0,1},{1,0},{6,7},{7,6},{8,9},{9,8},{14,15},{15,14},{16,17},{17,16... | collective-permute-start | bytes 798728 | tf_op jit(solution)/shard_map/ppermute | solution.py:790
  32.9 0.6 pad_add_fusion.refs_0_.where_at
  33.5 0.9 collective-permute-done.8.refs_10_
  34.4 0.7 copy-done.11
  35.1 40.5 %clip.1 = (bf16[80,1024]{1,0:T(8,128)(2,1)}, bf16[784,128]{1,0:T(8,128)(2,1)}, bf16[784,128]{1,0:T(8,128)(2,1)}, bf16[784,128]{1,0:T(8,128)(2,1)}, bf16[784,128]{1,0:T(8,128)(2,1)}) custom-call(s32[3]{0:T(128)} %pad_add_fusion.refs_0_.where_at, bf16[80,1664]{1,0:T(8,128)(2,1)} %pack.1.refs_1_, bf16[80,1664]{1,0:T(8,128)(2,1)} %copy-done.5, ...), custom_call_target="tpu_custom_call" | custom-call | flops 40000000000 | bytes 16777216 | tf_op jit(solution)/shard_map/clip/pallas_call | solution.py:854
  75.6 1.6 %collective-permute-start.9 = (bf16[784,128]{1,0:T(8,128)(2,1)}, bf16[784,128]{1,0:T(8,128)(2,1)S(1)}, u32[]{:S(2)}, u32[]{:S(2)}) collective-permute-start(bf16[784,128]{1,0:T(8,128)(2,1)} %get-tuple-element.9), channel_id=1, source_target_pairs={{0,8},{8,16},{16,24},{24,0},{1,9},{9,17},{17,25},{25,1},{2,10},{10... | collective-permute-start | bytes 602120 | tf_op jit(solution)/shard_map/ppermute | solution.py:815
  77.2 1.5 %collective-permute-start.10 = (bf16[784,128]{1,0:T(8,128)(2,1)}, bf16[784,128]{1,0:T(8,128)(2,1)S(1)}, u32[]{:S(2)}, u32[]{:S(2)}) collective-permute-start(bf16[784,128]{1,0:T(8,128)(2,1)} %get-tuple-element.10), channel_id=1, source_target_pairs={{0,16},{8,24},{16,0},{24,8},{1,17},{9,25},{17,1},{25,9},{2,18},{10... | collective-permute-start | bytes 602120 | tf_op jit(solution)/shard_map/ppermute | solution.py:815
  78.7 1.4 %collective-permute-start.11 = (bf16[784,128]{1,0:T(8,128)(2,1)}, bf16[784,128]{1,0:T(8,128)(2,1)S(1)}, u32[]{:S(2)}, u32[]{:S(2)}) collective-permute-start(bf16[784,128]{1,0:T(8,128)(2,1)} %get-tuple-element.11), channel_id=1, source_target_pairs={{0,24},{8,0},{16,8},{24,16},{1,25},{9,1},{17,9},{25,17},{2,26},{10... | collective-permute-start | bytes 602120 | tf_op jit(solution)/shard_map/ppermute | solution.py:815
  80.2 4.5 %collective-permute-done.9.refs_1_ = bf16[784,128]{1,0:T(8,128)(2,1)S(1)} collective-permute-done((bf16[784,128]{1,0:T(8,128)(2,1)}, bf16[784,128]{1,0:T(8,128)(2,1)S(1)}, u32[]{:S(2)}, u32[]{:S(2)}) %collective-permute-start.9) | collective-permute-done | bytes 200736 | tf_op jit(solution)/shard_map/ppermute | solution.py:815
  84.7 3.5 %collective-permute-done.10.refs_2_ = bf16[784,128]{1,0:T(8,128)(2,1)S(1)} collective-permute-done((bf16[784,128]{1,0:T(8,128)(2,1)}, bf16[784,128]{1,0:T(8,128)(2,1)S(1)}, u32[]{:S(2)}, u32[]{:S(2)}) %collective-permute-start.10) | collective-permute-done | bytes 200736 | tf_op jit(solution)/shard_map/ppermute | solution.py:815
  88.3 0.5 copy-done.1
  89.0 2.2 %join.1 = f32[784,128]{1,0:T(8,128)} custom-call(s32[3]{0:T(128)} %pad_add_fusion.refs_0_.where_at, bf16[784,128]{1,0:T(8,128)(2,1)} %get-tuple-element.8.refs_0_, bf16[784,128]{1,0:T(8,128)(2,1)} %copy-done, bf16[784,128]{1,0:T(8,128)(2,1)} %copy-done.1, bf16[784,128]{1,0:T(8,128)(2,1)} %copy-done.2), custom_call_target="tpu_custom_call" | custom-call | tf_op jit(solution)/shard_map/join/pallas_call | solution.py:912
  91.1 1.8 %slice.4 = f32[98368]{0:T(1024)} slice(f32[100352]{0:T(1024)} %bitcast.10), slice={[0:98368]} | slice | bytes 786944 | tf_op jit(solution)/shard_map/slice | solution.py:817
  (29 shorter events, 0.4 us)
Async XLA Ops:
  3.5 17.2 %collective-permute-start.1 = (bf16[80,1664]{1,0:T(8,128)(2,1)}, bf16[80,1664]{1,0:T(8,128)(2,1)S(1)}, u32[]{:S(2)}, u32[]{:S(2)}) collective-permute-start(bf16[80,1664]{1,0:T(8,128)(2,1)} %pack.1.refs_1_), channel_id=1, source_target_pairs={{4,0},{5,1},{6,2},{7,3},{0,4},{1,5},{2,6},{3,7},{12,8},{13,9},{14,... | collective-permute-start | bytes 798728 | tf_op jit(solution)/shard_map/ppermute | solution.py:787
  7.5 15.1 %collective-permute-start.2 = (bf16[80,1664]{1,0:T(8,128)(2,1)}, bf16[80,1664]{1,0:T(8,128)(2,1)S(1)}, u32[]{:S(2)}, u32[]{:S(2)}) collective-permute-start(bf16[80,1664]{1,0:T(8,128)(2,1)} %pack.1.refs_1_), channel_id=1, source_target_pairs={{0,2},{1,3},{2,4},{3,5},{4,6},{5,7},{8,10},{9,11},{10,12},{11,13},... | collective-permute-start | bytes 798728 | tf_op jit(solution)/shard_map/ppermute | solution.py:787
  11.0 14.7 %collective-permute-start = (bf16[80,1664]{1,0:T(8,128)(2,1)}, bf16[80,1664]{1,0:T(8,128)(2,1)S(1)}, u32[]{:S(2)}, u32[]{:S(2)}) collective-permute-start(bf16[80,1664]{1,0:T(8,128)(2,1)} %pack.1.refs_1_), channel_id=1, source_target_pairs={{2,0},{3,1},{4,2},{5,3},{6,4},{7,5},{10,8},{11,9},{12,10},{13,11},... | collective-permute-start | bytes 798728 | tf_op jit(solution)/shard_map/ppermute | solution.py:787
  20.7 13.6 %copy-start.3 = (bf16[80,1664]{1,0:T(8,128)(2,1)}, bf16[80,1664]{1,0:T(8,128)(2,1)S(1)}, u32[]{:S(2)}) copy-start(bf16[80,1664]{1,0:T(8,128)(2,1)S(1)} %collective-permute-done.1.refs_3_) | copy-start | bytes 798724
  20.7 10.2 %collective-permute-start.7 = (bf16[80,1664]{1,0:T(8,128)(2,1)S(1)}, bf16[80,1664]{1,0:T(8,128)(2,1)S(1)}, u32[]{:S(2)}, u32[]{:S(2)}) collective-permute-start(bf16[80,1664]{1,0:T(8,128)(2,1)S(1)} %collective-permute-done.1.refs_3_), channel_id=1, source_target_pairs={{2,0},{3,1},{4,6},{5,7},{10,8},{11,9},{12,14},{13,15},{18,16},{19,... | collective-permute-start | bytes 798728 | tf_op jit(solution)/shard_map/ppermute | solution.py:801
  22.0 11.4 %collective-permute-start.3 = (bf16[80,1664]{1,0:T(8,128)(2,1)}, bf16[80,1664]{1,0:T(8,128)(2,1)S(1)}, u32[]{:S(2)}, u32[]{:S(2)}) collective-permute-start(bf16[80,1664]{1,0:T(8,128)(2,1)} %pack.1.refs_1_), channel_id=1, source_target_pairs={{0,1},{1,0},{2,3},{3,2},{4,5},{5,4},{6,7},{7,6},{8,9},{9,8},{10,11... | collective-permute-start | bytes 798728 | tf_op jit(solution)/shard_map/ppermute | solution.py:790
  22.1 11.3 %collective-permute-start.5 = (bf16[80,1664]{1,0:T(8,128)(2,1)S(1)}, bf16[80,1664]{1,0:T(8,128)(2,1)S(1)}, u32[]{:S(2)}, u32[]{:S(2)}) collective-permute-start(bf16[80,1664]{1,0:T(8,128)(2,1)S(1)} %collective-permute-done.1.refs_3_), channel_id=1, source_target_pairs={{0,1},{1,0},{2,3},{3,2},{4,5},{5,4},{6,7},{7,6},{8,9},{9,8},{10,11... | collective-permute-start | bytes 798728 | tf_op jit(solution)/shard_map/ppermute | solution.py:790
  22.6 11.8 %copy-start.4 = (bf16[80,1664]{1,0:T(8,128)(2,1)}, bf16[80,1664]{1,0:T(8,128)(2,1)S(1)}, u32[]{:S(2)}) copy-start(bf16[80,1664]{1,0:T(8,128)(2,1)S(1)} %collective-permute-done.2.refs_4_) | copy-start | bytes 798724
  22.6 10.8 %collective-permute-start.6 = (bf16[80,1664]{1,0:T(8,128)(2,1)S(1)}, bf16[80,1664]{1,0:T(8,128)(2,1)S(1)}, u32[]{:S(2)}, u32[]{:S(2)}) collective-permute-start(bf16[80,1664]{1,0:T(8,128)(2,1)S(1)} %collective-permute-done.2.refs_4_), channel_id=1, source_target_pairs={{2,3},{3,2},{4,5},{5,4},{6,7},{7,6},{10,11},{11,10},{12,13},{13,12... | collective-permute-start | bytes 798728 | tf_op jit(solution)/shard_map/ppermute | solution.py:790
  25.7 8.6 %copy-start.5 = (bf16[80,1664]{1,0:T(8,128)(2,1)}, bf16[80,1664]{1,0:T(8,128)(2,1)S(1)}, u32[]{:S(2)}) copy-start(bf16[80,1664]{1,0:T(8,128)(2,1)S(1)} %collective-permute-done.refs_2_) | copy-start | bytes 798724
  25.7 7.7 %collective-permute-start.4 = (bf16[80,1664]{1,0:T(8,128)(2,1)S(1)}, bf16[80,1664]{1,0:T(8,128)(2,1)S(1)}, u32[]{:S(2)}, u32[]{:S(2)}) collective-permute-start(bf16[80,1664]{1,0:T(8,128)(2,1)S(1)} %collective-permute-done.refs_2_), channel_id=1, source_target_pairs={{0,1},{1,0},{2,3},{3,2},{4,5},{5,4},{8,9},{9,8},{10,11},{11,10},{1... | collective-permute-start | bytes 798728 | tf_op jit(solution)/shard_map/ppermute | solution.py:790
  30.9 3.4 %copy-start.6 = (bf16[80,1664]{1,0:T(8,128)(2,1)}, bf16[80,1664]{1,0:T(8,128)(2,1)S(1)}, u32[]{:S(2)}) copy-start(bf16[80,1664]{1,0:T(8,128)(2,1)S(1)} %collective-permute-done.7.refs_9_) | copy-start | bytes 798724
  30.9 3.4 %collective-permute-start.8 = (bf16[80,1664]{1,0:T(8,128)(2,1)S(1)}, bf16[80,1664]{1,0:T(8,128)(2,1)S(1)}, u32[]{:S(2)}, u32[]{:S(2)}) collective-permute-start(bf16[80,1664]{1,0:T(8,128)(2,1)S(1)} %collective-permute-done.7.refs_9_), channel_id=1, source_target_pairs={{0,1},{1,0},{6,7},{7,6},{8,9},{9,8},{14,15},{15,14},{16,17},{17,16... | collective-permute-start | bytes 798728 | tf_op jit(solution)/shard_map/ppermute | solution.py:790
  33.4 1.0 %copy-start.7 = (bf16[80,1664]{1,0:T(8,128)(2,1)}, bf16[80,1664]{1,0:T(8,128)(2,1)S(1)}, u32[]{:S(2)}) copy-start(bf16[80,1664]{1,0:T(8,128)(2,1)S(1)} %collective-permute-done.3.refs_5_) | copy-start | bytes 798724
  33.4 1.0 %copy-start.9 = (bf16[80,1664]{1,0:T(8,128)(2,1)}, bf16[80,1664]{1,0:T(8,128)(2,1)S(1)}, u32[]{:S(2)}) copy-start(bf16[80,1664]{1,0:T(8,128)(2,1)S(1)} %collective-permute-done.6.refs_8_) | copy-start | bytes 798724
  33.5 1.0 %copy-start.8 = (bf16[80,1664]{1,0:T(8,128)(2,1)}, bf16[80,1664]{1,0:T(8,128)(2,1)S(1)}, u32[]{:S(2)}) copy-start(bf16[80,1664]{1,0:T(8,128)(2,1)S(1)} %collective-permute-done.5.refs_7_) | copy-start | bytes 798724
  33.5 0.9 %copy-start.10 = (bf16[80,1664]{1,0:T(8,128)(2,1)}, bf16[80,1664]{1,0:T(8,128)(2,1)S(1)}, u32[]{:S(2)}) copy-start(bf16[80,1664]{1,0:T(8,128)(2,1)S(1)} %collective-permute-done.4.refs_6_) | copy-start | bytes 798724
  34.4 0.7 copy-start.11
  75.6 9.0 %collective-permute-start.9 = (bf16[784,128]{1,0:T(8,128)(2,1)}, bf16[784,128]{1,0:T(8,128)(2,1)S(1)}, u32[]{:S(2)}, u32[]{:S(2)}) collective-permute-start(bf16[784,128]{1,0:T(8,128)(2,1)} %get-tuple-element.9), channel_id=1, source_target_pairs={{0,8},{8,16},{16,24},{24,0},{1,9},{9,17},{17,25},{25,1},{2,10},{10... | collective-permute-start | bytes 602120 | tf_op jit(solution)/shard_map/ppermute | solution.py:815
  77.2 10.9 %collective-permute-start.10 = (bf16[784,128]{1,0:T(8,128)(2,1)}, bf16[784,128]{1,0:T(8,128)(2,1)S(1)}, u32[]{:S(2)}, u32[]{:S(2)}) collective-permute-start(bf16[784,128]{1,0:T(8,128)(2,1)} %get-tuple-element.10), channel_id=1, source_target_pairs={{0,16},{8,24},{16,0},{24,8},{1,17},{9,25},{17,1},{25,9},{2,18},{10... | collective-permute-start | bytes 602120 | tf_op jit(solution)/shard_map/ppermute | solution.py:815
  78.7 9.5 %collective-permute-start.11 = (bf16[784,128]{1,0:T(8,128)(2,1)}, bf16[784,128]{1,0:T(8,128)(2,1)S(1)}, u32[]{:S(2)}, u32[]{:S(2)}) collective-permute-start(bf16[784,128]{1,0:T(8,128)(2,1)} %get-tuple-element.11), channel_id=1, source_target_pairs={{0,24},{8,0},{16,8},{24,16},{1,25},{9,1},{17,9},{25,17},{2,26},{10... | collective-permute-start | bytes 602120 | tf_op jit(solution)/shard_map/ppermute | solution.py:815
  84.7 3.6 %copy-start = (bf16[784,128]{1,0:T(8,128)(2,1)}, bf16[784,128]{1,0:T(8,128)(2,1)S(1)}, u32[]{:S(2)}) copy-start(bf16[784,128]{1,0:T(8,128)(2,1)S(1)} %collective-permute-done.9.refs_1_) | copy-start | bytes 602116
  88.1 0.7 copy-start.1
  88.3 0.7 copy-start.2

commit v2 on v1

--- a/solution.py
+++ b/solution.py
@@ -302,14 +302,13 @@
     code = code + jnp.where(step >= step_at, float(SPOTS), 0.0)
     hits = (lax.broadcasted_iota(jnp.int32, (rows, count), 0) == slots[...]).astype(F32)
     covered = jnp.sum(hits, axis=1, keepdims=True)
+    masked = jnp.where((lane.astype(F32) == code) & (covered < 0.5), 1.0, 0.0).astype(BF16)
+    codes = jnp.sum(hits * (code[:, :count] + 1.0), axis=0, keepdims=True)
     hits = hits.astype(BF16)
-    masked = jnp.where((lane.astype(F32) == code) & (covered < 0.5), 1.0, 0.0).astype(BF16)
-    about = jnp.where(lane == 0, code + 1.0, 0.0).astype(BF16)
     out[:, :front] = tokens[...]
     out[:, front : front + width] = mm_tn(hits, cot[...]).astype(BF16)
     sums = mm_tn(masked, cot[...])[: 2 * SPOTS]
-    codes = mm_tn(about, hits)[:8]
-    codes = jnp.concatenate([codes, jnp.zeros((8, LANES - count), F32)], 1)
+    codes = jnp.concatenate([jnp.broadcast_to(codes, (8, count)), jnp.zeros((8, LANES - count), F32)], 1)
     rest = [sums[:, at * LANES : (at + 1) * LANES] for at in range(width // LANES)] + [codes]
     spare = count - 8 * len(rest)
     rest = jnp.concatenate(rest + [jnp.zeros((spare, LANES), F32)], 0)
@@ -324,16 +323,26 @@
     return places, at
 
 
-def store_flat(flat, widths, offset, which, lane_at, grad):
-    places, _ = flat_rows(widths)
-    stride = widths[which][1] // LANES
+def store_flat(flat, place, lanes, lane_at, grad):
     for at in range(grad.shape[1] // LANES):
         tile = grad[:, at * LANES : (at + 1) * LANES]
-        start = places[which] - offset + lane_at // LANES + at
+        start = place + lane_at // LANES + at
         if grad.shape[0] == 1:
             flat[start : start + 1, :] = tile
         else:
-            flat[pl.ds(start, grad.shape[0], stride=stride), :] = tile
+            flat[pl.ds(start, grad.shape[0], stride=lanes // LANES), :] = tile
+
+
+def head_rows(widths, n_dp, n_ctx):
+    places, total = flat_rows(widths)
+    block = total * LANES // (n_dp * n_ctx)
+    lanes = widths[1][1]
+    most = 0
+    for at in range(places[2] * LANES // block):
+        first = (at * block - places[1] * LANES) // lanes // PAD * PAD
+        last = ((at + 1) * block - places[1] * LANES - 1) // lanes
+        most = max(most, last + 1 - first)
+    return -(-most // PAD) * PAD
 
 
 def head_lanes(head, rows, lanes):
@@ -342,11 +351,10 @@
 
 
 def clip_kernel(n_dp, n_ctx, n_blocks, widths, *refs):
-    where_at = refs[0]
-    blocks = refs[1 : 1 + n_blocks]
-    enc_gain, mask_token, dec_gain = refs[1 + n_blocks : 4 + n_blocks]
-    far = refs[4 + n_blocks : 9 + n_blocks]
-    outs = refs[9 + n_blocks :]
+    blocks = refs[:n_blocks]
+    enc_gain, mask_token, dec_gain = refs[n_blocks : 3 + n_blocks]
+    far = refs[3 + n_blocks : 8 + n_blocks]
+    outs = refs[8 + n_blocks :]
     d_patches = outs[0]
     pieces = outs[1 : 1 + n_dp]
     (
@@ -373,6 +381,7 @@
         d_keys,
         d_values,
         d_latent,
+        d_res,
         d_mixed,
         turned,
         d_scores,
@@ -385,6 +394,7 @@
         dec_qkv_here,
         dec_out_here,
         flat,
+        part,
         cut,
         sems,
     ) = outs[1 + n_dp :]
@@ -393,7 +403,8 @@
         pltpu.make_async_copy(far[at], here[at], sems.at[at]) for at in range(len(here))
     ]
     loads[0].start()
-    core = where_at[0]
+    dp_at, ctx_at = lax.axis_index("dp"), lax.axis_index("ctx")
+    core = lax.rem(ctx_at, 2)
     count, width = blocks[0].shape[0], enc_gain.shape[1]
     slots = n_ctx * count
     chans = enc_out_here.shape[0]
@@ -411,7 +422,7 @@
     rest_at = slice(width + dec_width, width + dec_width + LANES)
 
     def pick(at, lanes):
-        chip = where_at[2] // 2
+        chip = ctx_at // 2
         block = blocks[at][:, lanes]
         hop = at % half
         if n_blocks == n_ctx or hop not in (1, half - 1):
@@ -436,7 +447,8 @@
     for at in range(3 * groups):
         lanes = slice(at * group_lanes, (at + 1) * group_lanes)
         qkv[:, lanes] = mm(nrm[...], enc_qkv_here[:, lanes]).astype(BF16)
-    nrm_t[...] = nrm[...].T
+    nrm_t[:PAD, :] = jnp.zeros((PAD, slots), BF16)
+    nrm_t[PAD:, :] = nrm[...].T
 
     def lanes_of(group):
         return [
@@ -604,8 +616,10 @@
         d_keys[shard] = mm_tn(d_score, q_stack[here, :]).astype(BF16)
         d_values[shard] = mm_tn(p_stack[here, :], d_stack[here, :]).astype(BF16)
 
-    def two_shards(at, carry):
-        both = [(2 * at + one, slice(one * tall, (one + 1) * tall)) for one in range(2)]
+    at_once = 4 if n_ctx % 4 == 0 else 2
+
+    def some_shards(at, carry):
+        both = [(at_once * at + one, slice(one * tall, (one + 1) * tall)) for one in range(at_once)]
         for shard, here in both:
             score(shard, here)
         soften()
@@ -616,7 +630,7 @@
             mix_back(shard, here)
         return carry
 
-    lax.fori_loop(0, half, two_shards, 0)
+    lax.fori_loop(0, n_ctx // at_once, some_shards, 0)
 
     mask_d_query = jnp.zeros((1, dec_chans), F32)
     mask_d_pair = [jnp.zeros((1, dec_chans), F32) for _ in range(2)]
@@ -657,12 +671,15 @@
             for shard in range(n_ctx):
                 d_latent[rows_of(place(shard, on_core)), :] = dec_in[rows_of(shard), :]
 
-    d_res = nrm
     d_res[...] = mm_nt(d_latent[...], enc_to_dec_here[...]).astype(BF16)
     d_mixed[...] = mm_nt(d_res[...], enc_out_here[...]).astype(BF16)
 
+    places, total = flat_rows(widths)
+    block_rows = 2 * total // (n_dp * n_ctx)
+    late_at = places[2]
+
     def store(which, lane_at, grad):
-        store_flat(flat, widths, 0, which, lane_at, grad)
+        store_flat(flat, places[which] - late_at, widths[which][1], lane_at, grad)
 
     store(2, 0, mm_tn(mixed[...], d_res[...]))
     store(3, 0, mm_tn(res[...], d_latent[...]))
@@ -696,67 +713,75 @@
             to_value = pl.ds(pl.multiple_of(chans + at_head * HEAD, HEAD), HEAD)
             query_t = turned[head * HEAD : (head + 1) * HEAD, :]
             cot_t = turned[group_lanes + head * HEAD : group_lanes + (head + 1) * HEAD, :]
-            d_kv_t[to_key, :] = mm(query_t, d_scores[head % 2]) * scale
-            d_kv_t[to_value, :] = mm(cot_t, weights[at_head])
+            d_kv_t[to_key, :] = (mm(query_t, d_scores[head % 2]) * scale).astype(BF16)
+            d_kv_t[to_value, :] = mm(cot_t, weights[at_head]).astype(BF16)
         return carry
 
     lax.fori_loop(0, groups, attend_back, 0)
-    d_qkv[:, chans:] = d_kv_t[...].T.astype(BF16)
-
-    places, total = flat_rows(widths)
-    gain_sum = jnp.zeros((width, LANES), F32)
-    for at in range(3 * groups):
-        lanes = slice(at * group_lanes, (at + 1) * group_lanes)
-        grad = mm(nrm_t[...], d_qkv[:, lanes])
-        store(1, at * group_lanes, grad)
-        weighed = grad * enc_qkv_here[:, lanes].astype(F32)
-        for to in range(group_lanes // LANES):
-            gain_sum += weighed[:, to * LANES : (to + 1) * LANES]
-    store(0, 0, jnp.sum(gain_sum.T, axis=0, keepdims=True) / enc_gain[...])
-    d_own = mm_nt(d_qkv[:count, :], enc_qkv_here[...])
+    d_qkv[:, chans:] = d_kv_t[...].T
+
+    d_nrm = mm_nt(d_qkv[...], enc_qkv_here[...])
+    gain_grad = jnp.sum(d_nrm * nrm[...].astype(F32), axis=0, keepdims=True) / enc_gain[...]
     unit, unit_scale = normed_rows(blocks[0][:, tokens_at].astype(F32))
-    d_own = norm_back(d_own, unit, unit_scale, enc_gain[...]).astype(BF16).astype(F32)
+    d_own = norm_back(d_nrm[:count], unit, unit_scale, enc_gain[...]).astype(BF16).astype(F32)
     d_patches[...] = (d_res[:count, :].astype(F32) + d_own).astype(BF16)
 
     piece_rows = cut.shape[1]
-    half_rows = 2 * total // (n_dp * n_ctx)
-
-    def cut_piece(to, carry):
-        start = (to * n_ctx + where_at[2]) * half_rows // 2
-        slot = lax.rem(to - where_at[1] + n_dp, n_dp)
+    some = head_rows(widths, n_dp, n_ctx)
+    lanes_all = 3 * chans
+    tiles = lanes_all // LANES
+
+    def cut_at(ref, start, to):
+        slot = lax.rem(to - dp_at + n_dp, n_dp)
         shift = lax.rem(start, 8)
         base = start - shift
         for small in range(8):
 
             @pl.when(shift == small)
             def _():
-                rows = flat[pl.ds(pl.multiple_of(base, 8), piece_rows + 8), :]
+                rows = ref[pl.ds(pl.multiple_of(base, 8), piece_rows + 8), :]
                 cut[slot] = rows[small : small + piece_rows].astype(BF16)
 
+    def cut_early(to, carry):
+        start = (to * n_ctx + ctx_at) * block_rows // 2
+        first = (start - places[1] + PAD * tiles) // tiles // PAD * PAD
+        rows = nrm_t[pl.ds(pl.multiple_of(first, PAD), some), :]
+        store_flat(part, 0, lanes_all, 0, mm(rows, d_qkv[...]))
+        begin = start - places[1] + (PAD - first) * tiles
+
+        @pl.when(start == 0)
+        def _():
+            store_flat(part, PAD * tiles - places[1], width, 0, gain_grad)
+
+        cut_at(part, begin, to)
         return carry
 
-    lax.fori_loop(0, n_dp, cut_piece, 0)
+    def cut_late(to, carry):
+        cut_at(flat, (to * n_ctx + ctx_at) * block_rows // 2 - late_at, to)
+        return carry
+
+    first_late = late_at * n_dp // total
+    lax.fori_loop(0, first_late, cut_early, 0)
+    lax.fori_loop(first_late, n_dp, cut_late, 0)
     for at in range(n_dp):
         pieces[at][...] = cut[at]
 
 
-def join_kernel(where_at, *refs):
+def join_kernel(*refs):
     out = refs[-1]
     total = refs[0][...].astype(F32)
     for ref in refs[1:-1]:
         total = total + ref[...].astype(F32)
-    rows = out.shape[0]
-    odd = lax.rem(where_at[2], 2) == 1
-
-    @pl.when(odd)
-    def _():
-        turned = pltpu.roll(total, LANES // 2, 1)
-        lane = lax.broadcasted_iota(jnp.int32, (rows, LANES), 1)
-        out[...] = jnp.where(lane < LANES // 2, turned, pltpu.roll(turned, rows - 1, 0))
-
-    @pl.when(jnp.logical_not(odd))
-    def _():
-        out[...] = total
+    rows = total.shape[0]
+    lane = lax.broadcasted_iota(jnp.int32, (rows, LANES), 1)
+    turned = pltpu.roll(total, LANES // 2, 1)
+    turned = jnp.where(lane < LANES // 2, turned, pltpu.roll(turned, rows - 1, 0))
+    total = jnp.where(lax.rem(lax.axis_index("ctx"), 2) == 1, turned, total)
+    full = out.shape[0] // (8 * LANES) * 8
+    left = out.shape[0] - full * LANES
+    out[: full * LANES] = total[:full].reshape(full * LANES)
+    if left > 0:
+        out[full * LANES :] = total[full : full + 8].reshape(8 * LANES)[:left]
 
 
 def fused_body(
@@ -806,15 +831,13 @@
         return near[:4] + far[:4] + [near[4], far[4]]
 
     blocks = by_hops(call_pack(shifts, tokens, vis_index, dec_cot[0]))
-    dp_at, ctx_at = lax.axis_index("dp"), lax.axis_index("ctx")
-    where_at = jnp.stack([ctx_at % 2, dp_at, ctx_at]).astype(jnp.int32)
-    d_patches, *pieces = call_clip(n_dp, n_ctx, widths, where_at, blocks, params)
+    d_patches, *pieces = call_clip(n_dp, n_ctx, widths, blocks, params)
     got = [pieces[0]]
     for step in range(1, n_dp):
         turn = [(at, (at + step) % n_dp) for at in range(n_dp)]
         got.append(lax.ppermute(pieces[step], "dp", turn))
     share = flat_rows(widths)[1] * LANES // (n_dp * n_ctx)
-    return d_patches[None], call_join(where_at, got).reshape(-1)[:share]
+    return d_patches[None], call_join(got, share)
 
 
 def piece_shape(n_dp, n_ctx, widths):
@@ -839,14 +862,15 @@
     )(shifts, tokens, vis_index, cot)
 
 
-def call_clip(n_dp, n_ctx, widths, where_at, blocks, params):
+def call_clip(n_dp, n_ctx, widths, blocks, params):
     enc_gain, enc_qkv, enc_out, enc_to_dec, mask_token, dec_gain, dec_qkv, dec_out = params
     count, width = blocks[0].shape[0], enc_gain.shape[0]
     slots = n_ctx * count
     chans = enc_out.shape[0]
     dec_chans, dec_width = dec_out.shape
-    total = flat_rows(widths)[1]
+    places, total = flat_rows(widths)
     piece = piece_shape(n_dp, n_ctx, widths)
+    part_rows = (head_rows(widths, n_dp, n_ctx) + PAD) * 3 * chans // LANES + 2 * PAD
     size = count + PAD
     tall = dec_chans // HEAD * size
     reach = 3 * count + PAD
@@ -854,11 +878,11 @@
     return pl.pallas_call(
         functools.partial(clip_kernel, n_dp, n_ctx, len(blocks), widths),
         out_shape=[jax.ShapeDtypeStruct((count, width), BF16)] + [piece] * n_dp,
-        in_specs=[IN_SMEM] + [IN_VMEM] * (len(blocks) + 3) + [ANYWHERE] * len(matrices),
+        in_specs=[IN_VMEM] * (len(blocks) + 3) + [ANYWHERE] * len(matrices),
         out_specs=[IN_VMEM] * (1 + n_dp),
         scratch_shapes=[
             pltpu.VMEM((slots, width), BF16),
-            pltpu.VMEM((width, slots), BF16),
+            pltpu.VMEM((PAD + width, slots), BF16),
             pltpu.VMEM((slots, 3 * chans), BF16),
             pltpu.VMEM((chans // HEAD, slots, slots), BF16),
             pltpu.VMEM((slots, chans), BF16),
@@ -871,25 +895,27 @@
             pltpu.VMEM((slots + PAD, 3 * dec_chans), BF16),
             pltpu.VMEM((n_ctx * size, dec_chans), BF16),
             pltpu.VMEM((n_ctx * size, dec_width), BF16),
-            pltpu.VMEM((2 * tall, reach), F32),
-            pltpu.VMEM((2 * tall, dec_chans), BF16),
-            pltpu.VMEM((2 * tall, dec_chans), BF16),
-            pltpu.VMEM((2 * tall, reach), BF16),
-            pltpu.VMEM((2 * tall, reach), BF16),
+            pltpu.VMEM((4 * tall, reach), F32),
+            pltpu.VMEM((4 * tall, dec_chans), BF16),
+            pltpu.VMEM((4 * tall, dec_chans), BF16),
+            pltpu.VMEM((4 * tall, reach), BF16),
+            pltpu.VMEM((4 * tall, reach), BF16),
             pltpu.VMEM((n_ctx * size, dec_chans), F32),
             pltpu.VMEM((n_ctx, reach, dec_chans), BF16),
             pltpu.VMEM((n_ctx, reach, dec_chans), BF16),
             pltpu.VMEM((slots, dec_width), BF16),
+            pltpu.VMEM((slots, width), BF16),
             pltpu.VMEM((slots, chans), BF16),
             pltpu.VMEM((8 * HEAD, slots), BF16),
             pltpu.VMEM((2, slots, slots), BF16),
-            pltpu.VMEM((2 * chans, slots), F32),
+            pltpu.VMEM((2 * chans, slots), BF16),
             pltpu.VMEM((slots, 3 * chans), BF16),
             pltpu.VMEM((8, slots), F32),
         ]
         + [pltpu.VMEM(matrix.shape, BF16) for matrix in matrices]
         + [
-            pltpu.VMEM((total + 2 * PAD, LANES), F32),
+            pltpu.VMEM((total - places[2] + 2 * PAD, LANES), F32),
+            pltpu.VMEM((part_rows, LANES), F32),
             pltpu.VMEM((n_dp,) + piece.shape, BF16),
             pltpu.SemaphoreType.DMA((len(matrices),)),
         ],
@@ -899,7 +925,6 @@
         ),
         name="clip",
     )(
-        where_at,
         *blocks,
         enc_gain[None],
         mask_token[None],
@@ -908,16 +933,18 @@
     )
 
 
-def call_join(where_at, blocks):
+def call_join(blocks, share):
     return pl.pallas_call(
         join_kernel,
-        out_shape=jax.ShapeDtypeStruct(blocks[0].shape, F32),
-        in_specs=[IN_SMEM] + [IN_VMEM] * len(blocks),
+        out_shape=jax.ShapeDtypeStruct((share,), F32),
+        in_specs=[IN_VMEM] * len(blocks),
         out_specs=IN_VMEM,
+        compiler_params=pltpu.CompilerParams(vmem_limit_bytes=SMALL_VMEM_BYTES),
         name="join",
-    )(where_at, *blocks)
-
-
+    )(*blocks)
+
+
+SMALL_VMEM_BYTES = 8 * 1024 * 1024
 VMEM_BYTES = 56 * 1024 * 1024
 
 

time: 93.3 us -> 88.5 us (0.949)
  Pallas kernels: 45.6 us -> 42.3 us
  local copies, waits for them, and re-layouts: 3.13 us -> 1.61 us
    pallas_call x1, Pallas kernels: 40.5 us -> 38.6 us  [call_clip(): pl.pallas_call(functools.partial(clip_kernel, n_dp, n_ctx, len(blocks), w...]
    slice x1 -> x0, local copies, waits for them, and re-layouts: 1.77 us -> none  [fused_body(): return (d_patches[None], call_join(where_at, got).reshape(-1)[:share])]
    pallas_call x1, Pallas kernels: 2.16 us -> 0.93 us  [call_join(): pl.pallas_call(join_kernel, out_shape=jax.ShapeDtypeStruct((share,), F32)...]
  transfers between devices with their start and end apart: 12 -> 12, of which waited for: 7 -> 7; matrix products, arithmetic and copies ran while one was open for 1% -> 0% of each run, Pallas kernels for 0% -> 0%
where the time goes in v2:
time: 88.5 us; the launch traced here: 88.2 us
  Pallas kernels  42.3 us (48%)
  waiting for transfers between devices  23.7 us (27%)
  starting transfers between devices  19.7 us (22%)
  local copies, waits for them, and re-layouts  1.61 us (2%)
    pallas_call x1, Pallas kernels, call_clip(): pl.pallas_call(functools.partial(clip_kernel, n_dp, n_ctx, len(blocks), w...  38.6 us
    ppermute x3, waiting for transfers between devices, shift(): return lax.ppermute(array, 'ctx', turn)  10.8 us
    ppermute x3, starting transfers between devices, shift(): return lax.ppermute(array, 'ctx', turn)  8.82 us
    ppermute x3, waiting for transfers between devices, fused_body(): got.append(lax.ppermute(pieces[step], 'dp', turn))  8.12 us
    ppermute x5, starting transfers between devices, swap(): lax.ppermute(array, 'ctx', [(2 * chip + core, 2 * chip + 1 - core) for ch...  5.05 us
    ppermute x3, starting transfers between devices, fused_body(): got.append(lax.ppermute(pieces[step], 'dp', turn))  4.55 us
    ppermute x1, waiting for transfers between devices, by_hops(): lax.ppermute(middle, 'ctx', [(2 * a + core, 2 * b + core) for a, b in ((1...  3.29 us
    pallas_call x1, Pallas kernels, call_pack(): pl.pallas_call(pack_kernel, out_shape=jax.ShapeDtypeStruct((count, width...  2.83 us
  transfers between devices with their start and end apart: 12, of which 7 were waited for; matrix products, arithmetic and copies ran while one was open for 0% of the time, Pallas kernels for 0%

profile of v2, /device:TPU:0, one launch (start us, length us, event | category | flops | bytes accessed | tf_op | source)
XLA Modules:
  0.0 88.2 jit_solution(18044526764368628680)
XLA Ops:
  0.6 2.8 %pack.1.refs_0_ = bf16[80,1664]{1,0:T(8,128)(2,1)} custom-call(s32[1,3]{1,0:T(1,128)} %shifts.1, bf16[80,1024]{1,0:T(8,128)(2,1)} %bitcast.7, s32[1,80]{1,0:T(1,128)} %slots.1, bf16[784,512]{1,0:T(8,128)(2,1)} %bitcast.6), custom_call_target="tpu_custom_call" | custom-call | tf_op jit(solution)/shard_map/pack/pallas_call | solution.py:856
  3.5 4.0 %collective-permute-start.1 = (bf16[80,1664]{1,0:T(8,128)(2,1)}, bf16[80,1664]{1,0:T(8,128)(2,1)S(1)}, u32[]{:S(2)}, u32[]{:S(2)}) collective-permute-start(bf16[80,1664]{1,0:T(8,128)(2,1)} %pack.1.refs_0_), channel_id=1, source_target_pairs={{4,0},{5,1},{6,2},{7,3},{0,4},{1,5},{2,6},{3,7},{12,8},{13,9},{14,... | collective-permute-start | bytes 798728 | tf_op jit(solution)/shard_map/ppermute | solution.py:812
  7.5 3.5 %collective-permute-start.2 = (bf16[80,1664]{1,0:T(8,128)(2,1)}, bf16[80,1664]{1,0:T(8,128)(2,1)S(1)}, u32[]{:S(2)}, u32[]{:S(2)}) collective-permute-start(bf16[80,1664]{1,0:T(8,128)(2,1)} %pack.1.refs_0_), channel_id=1, source_target_pairs={{0,2},{1,3},{2,4},{3,5},{4,6},{5,7},{8,10},{9,11},{10,12},{11,13},... | collective-permute-start | bytes 798728 | tf_op jit(solution)/shard_map/ppermute | solution.py:812
  11.0 1.3 %collective-permute-start = (bf16[80,1664]{1,0:T(8,128)(2,1)}, bf16[80,1664]{1,0:T(8,128)(2,1)S(1)}, u32[]{:S(2)}, u32[]{:S(2)}) collective-permute-start(bf16[80,1664]{1,0:T(8,128)(2,1)} %pack.1.refs_0_), channel_id=1, source_target_pairs={{2,0},{3,1},{4,2},{5,3},{6,4},{7,5},{10,8},{11,9},{12,10},{13,11},... | collective-permute-start | bytes 798728 | tf_op jit(solution)/shard_map/ppermute | solution.py:812
  12.3 8.4 %collective-permute-done.1.refs_2_ = bf16[80,1664]{1,0:T(8,128)(2,1)S(1)} collective-permute-done((bf16[80,1664]{1,0:T(8,128)(2,1)}, bf16[80,1664]{1,0:T(8,128)(2,1)S(1)}, u32[]{:S(2)}, u32[]{:S(2)}) %collective-permute-start.1) | collective-permute-done | bytes 266272 | tf_op jit(solution)/shard_map/ppermute | solution.py:812
  20.7 1.3 %collective-permute-start.7 = (bf16[80,1664]{1,0:T(8,128)(2,1)S(1)}, bf16[80,1664]{1,0:T(8,128)(2,1)S(1)}, u32[]{:S(2)}, u32[]{:S(2)}) collective-permute-start(bf16[80,1664]{1,0:T(8,128)(2,1)S(1)} %collective-permute-done.1.refs_2_), channel_id=1, source_target_pairs={{2,0},{3,1},{4,6},{5,7},{10,8},{11,9},{12,14},{13,15},{18,16},{19,... | collective-permute-start | bytes 798728 | tf_op jit(solution)/shard_map/ppermute | solution.py:826
  22.0 0.1 collective-permute-start.3
  22.1 0.5 collective-permute-start.5
  22.6 0.7 collective-permute-start.6
  23.2 2.4 %collective-permute-done.refs_1_ = bf16[80,1664]{1,0:T(8,128)(2,1)S(1)} collective-permute-done((bf16[80,1664]{1,0:T(8,128)(2,1)}, bf16[80,1664]{1,0:T(8,128)(2,1)S(1)}, u32[]{:S(2)}, u32[]{:S(2)}) %collective-permute-start) | collective-permute-done | bytes 266272 | tf_op jit(solution)/shard_map/ppermute | solution.py:812
  25.7 1.9 %collective-permute-start.4 = (bf16[80,1664]{1,0:T(8,128)(2,1)S(1)}, bf16[80,1664]{1,0:T(8,128)(2,1)S(1)}, u32[]{:S(2)}, u32[]{:S(2)}) collective-permute-start(bf16[80,1664]{1,0:T(8,128)(2,1)S(1)} %collective-permute-done.refs_1_), channel_id=1, source_target_pairs={{0,1},{1,0},{2,3},{3,2},{4,5},{5,4},{8,9},{9,8},{10,11},{11,10},{1... | collective-permute-start | bytes 798728 | tf_op jit(solution)/shard_map/ppermute | solution.py:815
  27.6 3.3 %collective-permute-done.7.refs_8_ = bf16[80,1664]{1,0:T(8,128)(2,1)S(1)} collective-permute-done((bf16[80,1664]{1,0:T(8,128)(2,1)S(1)}, bf16[80,1664]{1,0:T(8,128)(2,1)S(1)}, u32[]{:S(2)}, u32[]{:S(2)}) %collective-permute-start.7) | collective-permute-done | bytes 266272 | tf_op jit(solution)/shard_map/ppermute | solution.py:826
  30.9 1.9 %collective-permute-start.8 = (bf16[80,1664]{1,0:T(8,128)(2,1)S(1)}, bf16[80,1664]{1,0:T(8,128)(2,1)S(1)}, u32[]{:S(2)}, u32[]{:S(2)}) collective-permute-start(bf16[80,1664]{1,0:T(8,128)(2,1)S(1)} %collective-permute-done.7.refs_8_), channel_id=1, source_target_pairs={{0,1},{1,0},{6,7},{7,6},{8,9},{9,8},{14,15},{15,14},{16,17},{17,16... | collective-permute-start | bytes 798728 | tf_op jit(solution)/shard_map/ppermute | solution.py:815
  32.9 1.4 %collective-permute-done.8.refs_9_ = bf16[80,1664]{1,0:T(8,128)(2,1)S(1)} collective-permute-done((bf16[80,1664]{1,0:T(8,128)(2,1)S(1)}, bf16[80,1664]{1,0:T(8,128)(2,1)S(1)}, u32[]{:S(2)}, u32[]{:S(2)}) %collective-permute-start.8) | collective-permute-done | bytes 266272 | tf_op jit(solution)/shard_map/ppermute | solution.py:815
  34.4 0.6 copy-done.9
  35.0 38.6 %clip.1 = (bf16[80,1024]{1,0:T(8,128)(2,1)}, bf16[784,128]{1,0:T(8,128)(2,1)}, bf16[784,128]{1,0:T(8,128)(2,1)}, bf16[784,128]{1,0:T(8,128)(2,1)}, bf16[784,128]{1,0:T(8,128)(2,1)}) custom-call(bf16[80,1664]{1,0:T(8,128)(2,1)} %pack.1.refs_0_, bf16[80,1664]{1,0:T(8,128)(2,1)} %copy-done.3, bf16[80,1664]{1,0:T(8,128)(2,1)} %copy-done.1, ...), custom_call_target="tpu_custom_call" | custom-call | flops 40000000000 | bytes 16777216 | tf_op jit(solution)/shard_map/clip/pallas_call | solution.py:878
  73.6 1.6 %collective-permute-start.9 = (bf16[784,128]{1,0:T(8,128)(2,1)}, bf16[784,128]{1,0:T(8,128)(2,1)S(1)}, u32[]{:S(2)}, u32[]{:S(2)}) collective-permute-start(bf16[784,128]{1,0:T(8,128)(2,1)} %get-tuple-element.9), channel_id=1, source_target_pairs={{0,8},{8,16},{16,24},{24,0},{1,9},{9,17},{17,25},{25,1},{2,10},{10... | collective-permute-start | bytes 602120 | tf_op jit(solution)/shard_map/ppermute | solution.py:838
  75.2 1.5 %collective-permute-start.10 = (bf16[784,128]{1,0:T(8,128)(2,1)}, bf16[784,128]{1,0:T(8,128)(2,1)S(1)}, u32[]{:S(2)}, u32[]{:S(2)}) collective-permute-start(bf16[784,128]{1,0:T(8,128)(2,1)} %get-tuple-element.10), channel_id=1, source_target_pairs={{0,16},{8,24},{16,0},{24,8},{1,17},{9,25},{17,1},{25,9},{2,18},{10... | collective-permute-start | bytes 602120 | tf_op jit(solution)/shard_map/ppermute | solution.py:838
  76.7 1.4 %collective-permute-start.11 = (bf16[784,128]{1,0:T(8,128)(2,1)}, bf16[784,128]{1,0:T(8,128)(2,1)S(1)}, u32[]{:S(2)}, u32[]{:S(2)}) collective-permute-start(bf16[784,128]{1,0:T(8,128)(2,1)} %get-tuple-element.11), channel_id=1, source_target_pairs={{0,24},{8,0},{16,8},{24,16},{1,25},{9,1},{17,9},{25,17},{2,26},{10... | collective-permute-start | bytes 602120 | tf_op jit(solution)/shard_map/ppermute | solution.py:838
  78.2 4.5 %collective-permute-done.9.refs_1_ = bf16[784,128]{1,0:T(8,128)(2,1)S(1)} collective-permute-done((bf16[784,128]{1,0:T(8,128)(2,1)}, bf16[784,128]{1,0:T(8,128)(2,1)S(1)}, u32[]{:S(2)}, u32[]{:S(2)}) %collective-permute-start.9) | collective-permute-done | bytes 200736 | tf_op jit(solution)/shard_map/ppermute | solution.py:838
  82.6 3.5 %collective-permute-done.10.refs_2_ = bf16[784,128]{1,0:T(8,128)(2,1)S(1)} collective-permute-done((bf16[784,128]{1,0:T(8,128)(2,1)}, bf16[784,128]{1,0:T(8,128)(2,1)S(1)}, u32[]{:S(2)}, u32[]{:S(2)}) %collective-permute-start.10) | collective-permute-done | bytes 200736 | tf_op jit(solution)/shard_map/ppermute | solution.py:838
  86.1 0.2 collective-permute-done.11.refs_3_
  86.3 0.9 %copy-done = bf16[784,128]{1,0:T(8,128)(2,1)S(1)} copy-done((bf16[784,128]{1,0:T(8,128)(2,1)S(1)}, bf16[784,128]{1,0:T(8,128)(2,1)}, u32[]{:S(2)}) %copy-start) | copy-done | bytes 200728
  87.2 0.9 %join.1 = f32[98368]{0:T(1024)} custom-call(bf16[784,128]{1,0:T(8,128)(2,1)S(1)} %copy-done, bf16[784,128]{1,0:T(8,128)(2,1)S(1)} %collective-permute-done.9.refs_1_, bf16[784,128]{1,0:T(8,128)(2,1)S(1)} %collective-permute-done.10.refs_2_, bf16[784,128]{1,0:T(8,128)(2,1)S(1)} %collective-permute-done.11.refs_3_), custom_call_target="tpu_custom_call" | custom-call | tf_op jit(solution)/shard_map/join/pallas_call | solution.py:937
  (23 shorter events, 0.0 us)
Async XLA Ops:
  3.5 17.2 %collective-permute-start.1 = (bf16[80,1664]{1,0:T(8,128)(2,1)}, bf16[80,1664]{1,0:T(8,128)(2,1)S(1)}, u32[]{:S(2)}, u32[]{:S(2)}) collective-permute-start(bf16[80,1664]{1,0:T(8,128)(2,1)} %pack.1.refs_0_), channel_id=1, source_target_pairs={{4,0},{5,1},{6,2},{7,3},{0,4},{1,5},{2,6},{3,7},{12,8},{13,9},{14,... | collective-permute-start | bytes 798728 | tf_op jit(solution)/shard_map/ppermute | solution.py:812
  7.5 15.1 %collective-permute-start.2 = (bf16[80,1664]{1,0:T(8,128)(2,1)}, bf16[80,1664]{1,0:T(8,128)(2,1)S(1)}, u32[]{:S(2)}, u32[]{:S(2)}) collective-permute-start(bf16[80,1664]{1,0:T(8,128)(2,1)} %pack.1.refs_0_), channel_id=1, source_target_pairs={{0,2},{1,3},{2,4},{3,5},{4,6},{5,7},{8,10},{9,11},{10,12},{11,13},... | collective-permute-start | bytes 798728 | tf_op jit(solution)/shard_map/ppermute | solution.py:812
  11.0 14.7 %collective-permute-start = (bf16[80,1664]{1,0:T(8,128)(2,1)}, bf16[80,1664]{1,0:T(8,128)(2,1)S(1)}, u32[]{:S(2)}, u32[]{:S(2)}) collective-permute-start(bf16[80,1664]{1,0:T(8,128)(2,1)} %pack.1.refs_0_), channel_id=1, source_target_pairs={{2,0},{3,1},{4,2},{5,3},{6,4},{7,5},{10,8},{11,9},{12,10},{13,11},... | collective-permute-start | bytes 798728 | tf_op jit(solution)/shard_map/ppermute | solution.py:812
  20.7 13.6 %copy-start.1 = (bf16[80,1664]{1,0:T(8,128)(2,1)}, bf16[80,1664]{1,0:T(8,128)(2,1)S(1)}, u32[]{:S(2)}) copy-start(bf16[80,1664]{1,0:T(8,128)(2,1)S(1)} %collective-permute-done.1.refs_2_) | copy-start | bytes 798724
  20.7 10.2 %collective-permute-start.7 = (bf16[80,1664]{1,0:T(8,128)(2,1)S(1)}, bf16[80,1664]{1,0:T(8,128)(2,1)S(1)}, u32[]{:S(2)}, u32[]{:S(2)}) collective-permute-start(bf16[80,1664]{1,0:T(8,128)(2,1)S(1)} %collective-permute-done.1.refs_2_), channel_id=1, source_target_pairs={{2,0},{3,1},{4,6},{5,7},{10,8},{11,9},{12,14},{13,15},{18,16},{19,... | collective-permute-start | bytes 798728 | tf_op jit(solution)/shard_map/ppermute | solution.py:826
  22.0 10.8 %collective-permute-start.3 = (bf16[80,1664]{1,0:T(8,128)(2,1)}, bf16[80,1664]{1,0:T(8,128)(2,1)S(1)}, u32[]{:S(2)}, u32[]{:S(2)}) collective-permute-start(bf16[80,1664]{1,0:T(8,128)(2,1)} %pack.1.refs_0_), channel_id=1, source_target_pairs={{0,1},{1,0},{2,3},{3,2},{4,5},{5,4},{6,7},{7,6},{8,9},{9,8},{10,11... | collective-permute-start | bytes 798728 | tf_op jit(solution)/shard_map/ppermute | solution.py:815
  22.1 10.8 %collective-permute-start.5 = (bf16[80,1664]{1,0:T(8,128)(2,1)S(1)}, bf16[80,1664]{1,0:T(8,128)(2,1)S(1)}, u32[]{:S(2)}, u32[]{:S(2)}) collective-permute-start(bf16[80,1664]{1,0:T(8,128)(2,1)S(1)} %collective-permute-done.1.refs_2_), channel_id=1, source_target_pairs={{0,1},{1,0},{2,3},{3,2},{4,5},{5,4},{6,7},{7,6},{8,9},{9,8},{10,11... | collective-permute-start | bytes 798728 | tf_op jit(solution)/shard_map/ppermute | solution.py:815
  22.6 11.8 %copy-start.2 = (bf16[80,1664]{1,0:T(8,128)(2,1)}, bf16[80,1664]{1,0:T(8,128)(2,1)S(1)}, u32[]{:S(2)}) copy-start(bf16[80,1664]{1,0:T(8,128)(2,1)S(1)} %collective-permute-done.2.refs_3_) | copy-start | bytes 798724
  22.6 10.3 %collective-permute-start.6 = (bf16[80,1664]{1,0:T(8,128)(2,1)S(1)}, bf16[80,1664]{1,0:T(8,128)(2,1)S(1)}, u32[]{:S(2)}, u32[]{:S(2)}) collective-permute-start(bf16[80,1664]{1,0:T(8,128)(2,1)S(1)} %collective-permute-done.2.refs_3_), channel_id=1, source_target_pairs={{2,3},{3,2},{4,5},{5,4},{6,7},{7,6},{10,11},{11,10},{12,13},{13,12... | collective-permute-start | bytes 798728 | tf_op jit(solution)/shard_map/ppermute | solution.py:815
  25.7 8.6 %copy-start.3 = (bf16[80,1664]{1,0:T(8,128)(2,1)}, bf16[80,1664]{1,0:T(8,128)(2,1)S(1)}, u32[]{:S(2)}) copy-start(bf16[80,1664]{1,0:T(8,128)(2,1)S(1)} %collective-permute-done.refs_1_) | copy-start | bytes 798724
  25.7 7.2 %collective-permute-start.4 = (bf16[80,1664]{1,0:T(8,128)(2,1)S(1)}, bf16[80,1664]{1,0:T(8,128)(2,1)S(1)}, u32[]{:S(2)}, u32[]{:S(2)}) collective-permute-start(bf16[80,1664]{1,0:T(8,128)(2,1)S(1)} %collective-permute-done.refs_1_), channel_id=1, source_target_pairs={{0,1},{1,0},{2,3},{3,2},{4,5},{5,4},{8,9},{9,8},{10,11},{11,10},{1... | collective-permute-start | bytes 798728 | tf_op jit(solution)/shard_map/ppermute | solution.py:815
  30.9 3.4 %copy-start.4 = (bf16[80,1664]{1,0:T(8,128)(2,1)}, bf16[80,1664]{1,0:T(8,128)(2,1)S(1)}, u32[]{:S(2)}) copy-start(bf16[80,1664]{1,0:T(8,128)(2,1)S(1)} %collective-permute-done.7.refs_8_) | copy-start | bytes 798724
  30.9 3.4 %collective-permute-start.8 = (bf16[80,1664]{1,0:T(8,128)(2,1)S(1)}, bf16[80,1664]{1,0:T(8,128)(2,1)S(1)}, u32[]{:S(2)}, u32[]{:S(2)}) collective-permute-start(bf16[80,1664]{1,0:T(8,128)(2,1)S(1)} %collective-permute-done.7.refs_8_), channel_id=1, source_target_pairs={{0,1},{1,0},{6,7},{7,6},{8,9},{9,8},{14,15},{15,14},{16,17},{17,16... | collective-permute-start | bytes 798728 | tf_op jit(solution)/shard_map/ppermute | solution.py:815
  32.8 1.5 %copy-start.5 = (bf16[80,1664]{1,0:T(8,128)(2,1)}, bf16[80,1664]{1,0:T(8,128)(2,1)S(1)}, u32[]{:S(2)}) copy-start(bf16[80,1664]{1,0:T(8,128)(2,1)S(1)} %collective-permute-done.3.refs_4_) | copy-start | bytes 798724
  32.8 1.5 %copy-start.7 = (bf16[80,1664]{1,0:T(8,128)(2,1)}, bf16[80,1664]{1,0:T(8,128)(2,1)S(1)}, u32[]{:S(2)}) copy-start(bf16[80,1664]{1,0:T(8,128)(2,1)S(1)} %collective-permute-done.6.refs_7_) | copy-start | bytes 798724
  32.9 1.5 %copy-start.6 = (bf16[80,1664]{1,0:T(8,128)(2,1)}, bf16[80,1664]{1,0:T(8,128)(2,1)S(1)}, u32[]{:S(2)}) copy-start(bf16[80,1664]{1,0:T(8,128)(2,1)S(1)} %collective-permute-done.5.refs_6_) | copy-start | bytes 798724
  32.9 1.5 %copy-start.8 = (bf16[80,1664]{1,0:T(8,128)(2,1)}, bf16[80,1664]{1,0:T(8,128)(2,1)S(1)}, u32[]{:S(2)}) copy-start(bf16[80,1664]{1,0:T(8,128)(2,1)S(1)} %collective-permute-done.4.refs_5_) | copy-start | bytes 798724
  34.3 0.7 copy-start.9
  73.6 9.0 %collective-permute-start.9 = (bf16[784,128]{1,0:T(8,128)(2,1)}, bf16[784,128]{1,0:T(8,128)(2,1)S(1)}, u32[]{:S(2)}, u32[]{:S(2)}) collective-permute-start(bf16[784,128]{1,0:T(8,128)(2,1)} %get-tuple-element.9), channel_id=1, source_target_pairs={{0,8},{8,16},{16,24},{24,0},{1,9},{9,17},{17,25},{25,1},{2,10},{10... | collective-permute-start | bytes 602120 | tf_op jit(solution)/shard_map/ppermute | solution.py:838
  75.2 10.9 %collective-permute-start.10 = (bf16[784,128]{1,0:T(8,128)(2,1)}, bf16[784,128]{1,0:T(8,128)(2,1)S(1)}, u32[]{:S(2)}, u32[]{:S(2)}) collective-permute-start(bf16[784,128]{1,0:T(8,128)(2,1)} %get-tuple-element.10), channel_id=1, source_target_pairs={{0,16},{8,24},{16,0},{24,8},{1,17},{9,25},{17,1},{25,9},{2,18},{10... | collective-permute-start | bytes 602120 | tf_op jit(solution)/shard_map/ppermute | solution.py:838
  76.7 9.6 %collective-permute-start.11 = (bf16[784,128]{1,0:T(8,128)(2,1)}, bf16[784,128]{1,0:T(8,128)(2,1)S(1)}, u32[]{:S(2)}, u32[]{:S(2)}) collective-permute-start(bf16[784,128]{1,0:T(8,128)(2,1)} %get-tuple-element.11), channel_id=1, source_target_pairs={{0,24},{8,0},{16,8},{24,16},{1,25},{9,1},{17,9},{25,17},{2,26},{10... | collective-permute-start | bytes 602120 | tf_op jit(solution)/shard_map/ppermute | solution.py:838
  86.3 0.9 %copy-start = (bf16[784,128]{1,0:T(8,128)(2,1)S(1)}, bf16[784,128]{1,0:T(8,128)(2,1)}, u32[]{:S(2)}) copy-start(bf16[784,128]{1,0:T(8,128)(2,1)} %get-tuple-element.8.refs_0_) | copy-start | bytes 602116

commit v3 on v2

--- a/solution.py
+++ b/solution.py
@@ -440,9 +440,9 @@
         nrm[rows, :] = (unit * enc_gain[...]).astype(BF16)
         codes = codes_of(pick(at, rest_at).astype(F32))[:1]
         bias[:, rows] = jnp.broadcast_to(jnp.where(codes > 0.5, 0.0, NEG), (8, count))
+    loads[0].wait()
     for load in loads[1:]:
         load.start()
-    loads[0].wait()
 
     for at in range(3 * groups):
         lanes = slice(at * group_lanes, (at + 1) * group_lanes)
@@ -475,7 +475,8 @@
                 mixed[rows, lanes] = mix.astype(BF16)
         return carry
 
-    lax.fori_loop(0, groups, attend, 0)
+    for group in range(groups):
+        attend(group, 0)
 
     loads[1].wait()
     loads[2].wait()
@@ -616,7 +617,7 @@
         d_keys[shard] = mm_tn(d_score, q_stack[here, :]).astype(BF16)
         d_values[shard] = mm_tn(p_stack[here, :], d_stack[here, :]).astype(BF16)
 
-    at_once = 4 if n_ctx % 4 == 0 else 2
+    at_once = n_ctx
 
     def some_shards(at, carry):
         both = [(at_once * at + one, slice(one * tall, (one + 1) * tall)) for one in range(at_once)]
@@ -630,7 +631,7 @@
             mix_back(shard, here)
         return carry
 
-    lax.fori_loop(0, n_ctx // at_once, some_shards, 0)
+    some_shards(0, 0)
 
     mask_d_query = jnp.zeros((1, dec_chans), F32)
     mask_d_pair = [jnp.zeros((1, dec_chans), F32) for _ in range(2)]
@@ -717,7 +718,8 @@
             d_kv_t[to_value, :] = mm(cot_t, weights[at_head]).astype(BF16)
         return carry
 
-    lax.fori_loop(0, groups, attend_back, 0)
+    for group in range(groups):
+        attend_back(group, 0)
     d_qkv[:, chans:] = d_kv_t[...].T
 
     d_nrm = mm_nt(d_qkv[...], enc_qkv_here[...])
@@ -732,7 +734,7 @@
     tiles = lanes_all // LANES
 
     def cut_at(ref, start, to):
-        slot = lax.rem(to - dp_at + n_dp, n_dp)
+        slot = to ^ dp_at if n_dp & (n_dp - 1) == 0 else lax.rem(to - dp_at + n_dp, n_dp)
         shift = lax.rem(start, 8)
         base = start - shift
         for small in range(8):
@@ -834,7 +836,10 @@
     d_patches, *pieces = call_clip(n_dp, n_ctx, widths, blocks, params)
     got = [pieces[0]]
     for step in range(1, n_dp):
-        turn = [(at, (at + step) % n_dp) for at in range(n_dp)]
+        if n_dp & (n_dp - 1) == 0:
+            turn = [(at, at ^ step) for at in range(n_dp)]
+        else:
+            turn = [(at, (at + step) % n_dp) for at in range(n_dp)]
         got.append(lax.ppermute(pieces[step], "dp", turn))
     share = flat_rows(widths)[1] * LANES // (n_dp * n_ctx)
     return d_patches[None], call_join(got, share)
@@ -895,11 +900,11 @@
             pltpu.VMEM((slots + PAD, 3 * dec_chans), BF16),
             pltpu.VMEM((n_ctx * size, dec_chans), BF16),
             pltpu.VMEM((n_ctx * size, dec_width), BF16),
-            pltpu.VMEM((4 * tall, reach), F32),
-            pltpu.VMEM((4 * tall, dec_chans), BF16),
-            pltpu.VMEM((4 * tall, dec_chans), BF16),
-            pltpu.VMEM((4 * tall, reach), BF16),
-            pltpu.VMEM((4 * tall, reach), BF16),
+            pltpu.VMEM((n_ctx * tall, reach), F32),
+            pltpu.VMEM((n_ctx * tall, dec_chans), BF16),
+            pltpu.VMEM((n_ctx * tall, dec_chans), BF16),
+            pltpu.VMEM((n_ctx * tall, reach), BF16),
+            pltpu.VMEM((n_ctx * tall, reach), BF16),
             pltpu.VMEM((n_ctx * size, dec_chans), F32),
             pltpu.VMEM((n_ctx, reach, dec_chans), BF16),
             pltpu.VMEM((n_ctx, reach, dec_chans), BF16),

time: 88.5 us -> 85.7 us (0.968)
  Pallas kernels: 42.3 us -> 39.3 us
  waiting for transfers between devices: 23.7 us -> 24.9 us
  starting transfers between devices: 19.7 us -> 18.7 us
    pallas_call x1, Pallas kernels: 38.6 us -> 35.6 us  [call_clip(): pl.pallas_call(functools.partial(clip_kernel, n_dp, n_ctx, len(blocks), w...]
    ppermute x3, waiting for transfers between devices: 8.12 us -> 9.35 us  [fused_body(): got.append(lax.ppermute(pieces[step], 'dp', turn))]
    ppermute x3, starting transfers between devices: 4.55 us -> 3.55 us  [fused_body(): got.append(lax.ppermute(pieces[step], 'dp', turn))]
  transfers between devices with their start and end apart: 12 -> 12, of which waited for: 7 -> 6; matrix products, arithmetic and copies ran while one was open for 0% -> 0% of each run, Pallas kernels for 0% -> 0%
where the time goes in v3:
time: 85.7 us; the launch traced here: 85.4 us
  Pallas kernels  39.3 us (46%)
  waiting for transfers between devices  24.9 us (29%)
  starting transfers between devices  18.7 us (22%)
  local copies, waits for them, and re-layouts  1.61 us (2%)
    pallas_call x1, Pallas kernels, call_clip(): pl.pallas_call(functools.partial(clip_kernel, n_dp, n_ctx, len(blocks), w...  35.6 us
    ppermute x3, waiting for transfers between devices, shift(): return lax.ppermute(array, 'ctx', turn)  10.8 us
    ppermute x3, waiting for transfers between devices, fused_body(): got.append(lax.ppermute(pieces[step], 'dp', turn))  9.35 us
    ppermute x3, starting transfers between devices, shift(): return lax.ppermute(array, 'ctx', turn)  8.82 us
    ppermute x5, starting transfers between devices, swap(): lax.ppermute(array, 'ctx', [(2 * chip + core, 2 * chip + 1 - core) for ch...  5.05 us
    ppermute x3, starting transfers between devices, fused_body(): got.append(lax.ppermute(pieces[step], 'dp', turn))  3.55 us
    ppermute x1, waiting for transfers between devices, by_hops(): lax.ppermute(middle, 'ctx', [(2 * a + core, 2 * b + core) for a, b in ((1...  3.29 us
    pallas_call x1, Pallas kernels, call_pack(): pl.pallas_call(pack_kernel, out_shape=jax.ShapeDtypeStruct((count, width...  2.83 us
  transfers between devices with their start and end apart: 12, of which 6 were waited for; matrix products, arithmetic and copies ran while one was open for 0% of the time, Pallas kernels for 0%

profile of v3, /device:TPU:0, one launch (start us, length us, event | category | flops | bytes accessed | tf_op | source)
XLA Modules:
  0.0 85.4 jit_solution(11528579266940046201)
XLA Ops:
  0.6 2.8 %pack.1.refs_0_ = bf16[80,1664]{1,0:T(8,128)(2,1)} custom-call(s32[1,3]{1,0:T(1,128)} %shifts.1, bf16[80,1024]{1,0:T(8,128)(2,1)} %bitcast.7, s32[1,80]{1,0:T(1,128)} %slots.1, bf16[784,512]{1,0:T(8,128)(2,1)} %bitcast.6), custom_call_target="tpu_custom_call" | custom-call | tf_op jit(solution)/shard_map/pack/pallas_call | solution.py:861
  3.5 4.0 %collective-permute-start.1 = (bf16[80,1664]{1,0:T(8,128)(2,1)}, bf16[80,1664]{1,0:T(8,128)(2,1)S(1)}, u32[]{:S(2)}, u32[]{:S(2)}) collective-permute-start(bf16[80,1664]{1,0:T(8,128)(2,1)} %pack.1.refs_0_), channel_id=1, source_target_pairs={{4,0},{5,1},{6,2},{7,3},{0,4},{1,5},{2,6},{3,7},{12,8},{13,9},{14,... | collective-permute-start | bytes 798728 | tf_op jit(solution)/shard_map/ppermute | solution.py:814
  7.5 3.5 %collective-permute-start.2 = (bf16[80,1664]{1,0:T(8,128)(2,1)}, bf16[80,1664]{1,0:T(8,128)(2,1)S(1)}, u32[]{:S(2)}, u32[]{:S(2)}) collective-permute-start(bf16[80,1664]{1,0:T(8,128)(2,1)} %pack.1.refs_0_), channel_id=1, source_target_pairs={{0,2},{1,3},{2,4},{3,5},{4,6},{5,7},{8,10},{9,11},{10,12},{11,13},... | collective-permute-start | bytes 798728 | tf_op jit(solution)/shard_map/ppermute | solution.py:814
  11.0 1.3 %collective-permute-start = (bf16[80,1664]{1,0:T(8,128)(2,1)}, bf16[80,1664]{1,0:T(8,128)(2,1)S(1)}, u32[]{:S(2)}, u32[]{:S(2)}) collective-permute-start(bf16[80,1664]{1,0:T(8,128)(2,1)} %pack.1.refs_0_), channel_id=1, source_target_pairs={{2,0},{3,1},{4,2},{5,3},{6,4},{7,5},{10,8},{11,9},{12,10},{13,11},... | collective-permute-start | bytes 798728 | tf_op jit(solution)/shard_map/ppermute | solution.py:814
  12.3 8.4 %collective-permute-done.1.refs_2_ = bf16[80,1664]{1,0:T(8,128)(2,1)S(1)} collective-permute-done((bf16[80,1664]{1,0:T(8,128)(2,1)}, bf16[80,1664]{1,0:T(8,128)(2,1)S(1)}, u32[]{:S(2)}, u32[]{:S(2)}) %collective-permute-start.1) | collective-permute-done | bytes 266272 | tf_op jit(solution)/shard_map/ppermute | solution.py:814
  20.7 1.3 %collective-permute-start.7 = (bf16[80,1664]{1,0:T(8,128)(2,1)S(1)}, bf16[80,1664]{1,0:T(8,128)(2,1)S(1)}, u32[]{:S(2)}, u32[]{:S(2)}) collective-permute-start(bf16[80,1664]{1,0:T(8,128)(2,1)S(1)} %collective-permute-done.1.refs_2_), channel_id=1, source_target_pairs={{2,0},{3,1},{4,6},{5,7},{10,8},{11,9},{12,14},{13,15},{18,16},{19,... | collective-permute-start | bytes 798728 | tf_op jit(solution)/shard_map/ppermute | solution.py:828
  22.0 0.1 collective-permute-start.3
  22.1 0.5 collective-permute-start.5
  22.6 0.0 collective-permute-done.2.refs_3_
  22.6 0.7 collective-permute-start.6
  23.2 2.4 %collective-permute-done.refs_1_ = bf16[80,1664]{1,0:T(8,128)(2,1)S(1)} collective-permute-done((bf16[80,1664]{1,0:T(8,128)(2,1)}, bf16[80,1664]{1,0:T(8,128)(2,1)S(1)}, u32[]{:S(2)}, u32[]{:S(2)}) %collective-permute-start) | collective-permute-done | bytes 266272 | tf_op jit(solution)/shard_map/ppermute | solution.py:814
  25.7 1.9 %collective-permute-start.4 = (bf16[80,1664]{1,0:T(8,128)(2,1)S(1)}, bf16[80,1664]{1,0:T(8,128)(2,1)S(1)}, u32[]{:S(2)}, u32[]{:S(2)}) collective-permute-start(bf16[80,1664]{1,0:T(8,128)(2,1)S(1)} %collective-permute-done.refs_1_), channel_id=1, source_target_pairs={{0,1},{1,0},{2,3},{3,2},{4,5},{5,4},{8,9},{9,8},{10,11},{11,10},{1... | collective-permute-start | bytes 798728 | tf_op jit(solution)/shard_map/ppermute | solution.py:817
  27.6 3.3 %collective-permute-done.7.refs_8_ = bf16[80,1664]{1,0:T(8,128)(2,1)S(1)} collective-permute-done((bf16[80,1664]{1,0:T(8,128)(2,1)S(1)}, bf16[80,1664]{1,0:T(8,128)(2,1)S(1)}, u32[]{:S(2)}, u32[]{:S(2)}) %collective-permute-start.7) | collective-permute-done | bytes 266272 | tf_op jit(solution)/shard_map/ppermute | solution.py:828
  30.9 1.9 %collective-permute-start.8 = (bf16[80,1664]{1,0:T(8,128)(2,1)S(1)}, bf16[80,1664]{1,0:T(8,128)(2,1)S(1)}, u32[]{:S(2)}, u32[]{:S(2)}) collective-permute-start(bf16[80,1664]{1,0:T(8,128)(2,1)S(1)} %collective-permute-done.7.refs_8_), channel_id=1, source_target_pairs={{0,1},{1,0},{6,7},{7,6},{8,9},{9,8},{14,15},{15,14},{16,17},{17,16... | collective-permute-start | bytes 798728 | tf_op jit(solution)/shard_map/ppermute | solution.py:817
  32.9 1.4 %collective-permute-done.8.refs_9_ = bf16[80,1664]{1,0:T(8,128)(2,1)S(1)} collective-permute-done((bf16[80,1664]{1,0:T(8,128)(2,1)S(1)}, bf16[80,1664]{1,0:T(8,128)(2,1)S(1)}, u32[]{:S(2)}, u32[]{:S(2)}) %collective-permute-start.8) | collective-permute-done | bytes 266272 | tf_op jit(solution)/shard_map/ppermute | solution.py:817
  34.4 0.6 copy-done.9
  35.0 35.6 %clip.1 = (bf16[80,1024]{1,0:T(8,128)(2,1)}, bf16[784,128]{1,0:T(8,128)(2,1)}, bf16[784,128]{1,0:T(8,128)(2,1)}, bf16[784,128]{1,0:T(8,128)(2,1)}, bf16[784,128]{1,0:T(8,128)(2,1)}) custom-call(bf16[80,1664]{1,0:T(8,128)(2,1)} %pack.1.refs_0_, bf16[80,1664]{1,0:T(8,128)(2,1)} %copy-done.3, bf16[80,1664]{1,0:T(8,128)(2,1)} %copy-done.1, ...), custom_call_target="tpu_custom_call" | custom-call | flops 40000000000 | bytes 16777216 | tf_op jit(solution)/shard_map/clip/pallas_call | solution.py:883
  70.6 1.6 %collective-permute-start.9 = (bf16[784,128]{1,0:T(8,128)(2,1)}, bf16[784,128]{1,0:T(8,128)(2,1)S(1)}, u32[]{:S(2)}, u32[]{:S(2)}) collective-permute-start(bf16[784,128]{1,0:T(8,128)(2,1)} %get-tuple-element.9), channel_id=1, source_target_pairs={{0,8},{8,0},{16,24},{24,16},{1,9},{9,1},{17,25},{25,17},{2,10},{10... | collective-permute-start | bytes 602120 | tf_op jit(solution)/shard_map/ppermute | solution.py:843
  72.2 1.5 %collective-permute-start.10 = (bf16[784,128]{1,0:T(8,128)(2,1)}, bf16[784,128]{1,0:T(8,128)(2,1)S(1)}, u32[]{:S(2)}, u32[]{:S(2)}) collective-permute-start(bf16[784,128]{1,0:T(8,128)(2,1)} %get-tuple-element.10), channel_id=1, source_target_pairs={{0,16},{8,24},{16,0},{24,8},{1,17},{9,25},{17,1},{25,9},{2,18},{10... | collective-permute-start | bytes 602120 | tf_op jit(solution)/shard_map/ppermute | solution.py:843
  73.7 0.4 collective-permute-start.11
  74.2 4.6 %collective-permute-done.9.refs_1_ = bf16[784,128]{1,0:T(8,128)(2,1)S(1)} collective-permute-done((bf16[784,128]{1,0:T(8,128)(2,1)}, bf16[784,128]{1,0:T(8,128)(2,1)S(1)}, u32[]{:S(2)}, u32[]{:S(2)}) %collective-permute-start.9) | collective-permute-done | bytes 200736 | tf_op jit(solution)/shard_map/ppermute | solution.py:843
  78.7 4.8 %collective-permute-done.10.refs_2_ = bf16[784,128]{1,0:T(8,128)(2,1)S(1)} collective-permute-done((bf16[784,128]{1,0:T(8,128)(2,1)}, bf16[784,128]{1,0:T(8,128)(2,1)S(1)}, u32[]{:S(2)}, u32[]{:S(2)}) %collective-permute-start.10) | collective-permute-done | bytes 200736 | tf_op jit(solution)/shard_map/ppermute | solution.py:843
  83.5 0.9 %copy-done = bf16[784,128]{1,0:T(8,128)(2,1)S(1)} copy-done((bf16[784,128]{1,0:T(8,128)(2,1)S(1)}, bf16[784,128]{1,0:T(8,128)(2,1)}, u32[]{:S(2)}) %copy-start) | copy-done | bytes 200728
  84.4 0.9 %join.1 = f32[98368]{0:T(1024)} custom-call(bf16[784,128]{1,0:T(8,128)(2,1)S(1)} %copy-done, bf16[784,128]{1,0:T(8,128)(2,1)S(1)} %collective-permute-done.9.refs_1_, bf16[784,128]{1,0:T(8,128)(2,1)S(1)} %collective-permute-done.10.refs_2_, bf16[784,128]{1,0:T(8,128)(2,1)S(1)} %collective-permute-done.11.refs_3_), custom_call_target="tpu_custom_call" | custom-call | tf_op jit(solution)/shard_map/join/pallas_call | solution.py:942
  (23 shorter events, 0.0 us)
Async XLA Ops:
  3.5 17.2 %collective-permute-start.1 = (bf16[80,1664]{1,0:T(8,128)(2,1)}, bf16[80,1664]{1,0:T(8,128)(2,1)S(1)}, u32[]{:S(2)}, u32[]{:S(2)}) collective-permute-start(bf16[80,1664]{1,0:T(8,128)(2,1)} %pack.1.refs_0_), channel_id=1, source_target_pairs={{4,0},{5,1},{6,2},{7,3},{0,4},{1,5},{2,6},{3,7},{12,8},{13,9},{14,... | collective-permute-start | bytes 798728 | tf_op jit(solution)/shard_map/ppermute | solution.py:814
  7.5 15.1 %collective-permute-start.2 = (bf16[80,1664]{1,0:T(8,128)(2,1)}, bf16[80,1664]{1,0:T(8,128)(2,1)S(1)}, u32[]{:S(2)}, u32[]{:S(2)}) collective-permute-start(bf16[80,1664]{1,0:T(8,128)(2,1)} %pack.1.refs_0_), channel_id=1, source_target_pairs={{0,2},{1,3},{2,4},{3,5},{4,6},{5,7},{8,10},{9,11},{10,12},{11,13},... | collective-permute-start | bytes 798728 | tf_op jit(solution)/shard_map/ppermute | solution.py:814
  11.0 14.7 %collective-permute-start = (bf16[80,1664]{1,0:T(8,128)(2,1)}, bf16[80,1664]{1,0:T(8,128)(2,1)S(1)}, u32[]{:S(2)}, u32[]{:S(2)}) collective-permute-start(bf16[80,1664]{1,0:T(8,128)(2,1)} %pack.1.refs_0_), channel_id=1, source_target_pairs={{2,0},{3,1},{4,2},{5,3},{6,4},{7,5},{10,8},{11,9},{12,10},{13,11},... | collective-permute-start | bytes 798728 | tf_op jit(solution)/shard_map/ppermute | solution.py:814
  20.7 13.6 %copy-start.1 = (bf16[80,1664]{1,0:T(8,128)(2,1)}, bf16[80,1664]{1,0:T(8,128)(2,1)S(1)}, u32[]{:S(2)}) copy-start(bf16[80,1664]{1,0:T(8,128)(2,1)S(1)} %collective-permute-done.1.refs_2_) | copy-start | bytes 798724
  20.7 10.2 %collective-permute-start.7 = (bf16[80,1664]{1,0:T(8,128)(2,1)S(1)}, bf16[80,1664]{1,0:T(8,128)(2,1)S(1)}, u32[]{:S(2)}, u32[]{:S(2)}) collective-permute-start(bf16[80,1664]{1,0:T(8,128)(2,1)S(1)} %collective-permute-done.1.refs_2_), channel_id=1, source_target_pairs={{2,0},{3,1},{4,6},{5,7},{10,8},{11,9},{12,14},{13,15},{18,16},{19,... | collective-permute-start | bytes 798728 | tf_op jit(solution)/shard_map/ppermute | solution.py:828
  22.0 10.8 %collective-permute-start.3 = (bf16[80,1664]{1,0:T(8,128)(2,1)}, bf16[80,1664]{1,0:T(8,128)(2,1)S(1)}, u32[]{:S(2)}, u32[]{:S(2)}) collective-permute-start(bf16[80,1664]{1,0:T(8,128)(2,1)} %pack.1.refs_0_), channel_id=1, source_target_pairs={{0,1},{1,0},{2,3},{3,2},{4,5},{5,4},{6,7},{7,6},{8,9},{9,8},{10,11... | collective-permute-start | bytes 798728 | tf_op jit(solution)/shard_map/ppermute | solution.py:817
  22.1 10.8 %collective-permute-start.5 = (bf16[80,1664]{1,0:T(8,128)(2,1)S(1)}, bf16[80,1664]{1,0:T(8,128)(2,1)S(1)}, u32[]{:S(2)}, u32[]{:S(2)}) collective-permute-start(bf16[80,1664]{1,0:T(8,128)(2,1)S(1)} %collective-permute-done.1.refs_2_), channel_id=1, source_target_pairs={{0,1},{1,0},{2,3},{3,2},{4,5},{5,4},{6,7},{7,6},{8,9},{9,8},{10,11... | collective-permute-start | bytes 798728 | tf_op jit(solution)/shard_map/ppermute | solution.py:817
  22.6 11.8 %copy-start.2 = (bf16[80,1664]{1,0:T(8,128)(2,1)}, bf16[80,1664]{1,0:T(8,128)(2,1)S(1)}, u32[]{:S(2)}) copy-start(bf16[80,1664]{1,0:T(8,128)(2,1)S(1)} %collective-permute-done.2.refs_3_) | copy-start | bytes 798724
  22.6 10.3 %collective-permute-start.6 = (bf16[80,1664]{1,0:T(8,128)(2,1)S(1)}, bf16[80,1664]{1,0:T(8,128)(2,1)S(1)}, u32[]{:S(2)}, u32[]{:S(2)}) collective-permute-start(bf16[80,1664]{1,0:T(8,128)(2,1)S(1)} %collective-permute-done.2.refs_3_), channel_id=1, source_target_pairs={{2,3},{3,2},{4,5},{5,4},{6,7},{7,6},{10,11},{11,10},{12,13},{13,12... | collective-permute-start | bytes 798728 | tf_op jit(solution)/shard_map/ppermute | solution.py:817
  25.7 8.6 %copy-start.3 = (bf16[80,1664]{1,0:T(8,128)(2,1)}, bf16[80,1664]{1,0:T(8,128)(2,1)S(1)}, u32[]{:S(2)}) copy-start(bf16[80,1664]{1,0:T(8,128)(2,1)S(1)} %collective-permute-done.refs_1_) | copy-start | bytes 798724
  25.7 7.2 %collective-permute-start.4 = (bf16[80,1664]{1,0:T(8,128)(2,1)S(1)}, bf16[80,1664]{1,0:T(8,128)(2,1)S(1)}, u32[]{:S(2)}, u32[]{:S(2)}) collective-permute-start(bf16[80,1664]{1,0:T(8,128)(2,1)S(1)} %collective-permute-done.refs_1_), channel_id=1, source_target_pairs={{0,1},{1,0},{2,3},{3,2},{4,5},{5,4},{8,9},{9,8},{10,11},{11,10},{1... | collective-permute-start | bytes 798728 | tf_op jit(solution)/shard_map/ppermute | solution.py:817
  30.9 3.4 %copy-start.4 = (bf16[80,1664]{1,0:T(8,128)(2,1)}, bf16[80,1664]{1,0:T(8,128)(2,1)S(1)}, u32[]{:S(2)}) copy-start(bf16[80,1664]{1,0:T(8,128)(2,1)S(1)} %collective-permute-done.7.refs_8_) | copy-start | bytes 798724
  30.9 3.4 %collective-permute-start.8 = (bf16[80,1664]{1,0:T(8,128)(2,1)S(1)}, bf16[80,1664]{1,0:T(8,128)(2,1)S(1)}, u32[]{:S(2)}, u32[]{:S(2)}) collective-permute-start(bf16[80,1664]{1,0:T(8,128)(2,1)S(1)} %collective-permute-done.7.refs_8_), channel_id=1, source_target_pairs={{0,1},{1,0},{6,7},{7,6},{8,9},{9,8},{14,15},{15,14},{16,17},{17,16... | collective-permute-start | bytes 798728 | tf_op jit(solution)/shard_map/ppermute | solution.py:817
  32.8 1.5 %copy-start.5 = (bf16[80,1664]{1,0:T(8,128)(2,1)}, bf16[80,1664]{1,0:T(8,128)(2,1)S(1)}, u32[]{:S(2)}) copy-start(bf16[80,1664]{1,0:T(8,128)(2,1)S(1)} %collective-permute-done.3.refs_4_) | copy-start | bytes 798724
  32.8 1.5 %copy-start.7 = (bf16[80,1664]{1,0:T(8,128)(2,1)}, bf16[80,1664]{1,0:T(8,128)(2,1)S(1)}, u32[]{:S(2)}) copy-start(bf16[80,1664]{1,0:T(8,128)(2,1)S(1)} %collective-permute-done.6.refs_7_) | copy-start | bytes 798724
  32.9 1.5 %copy-start.6 = (bf16[80,1664]{1,0:T(8,128)(2,1)}, bf16[80,1664]{1,0:T(8,128)(2,1)S(1)}, u32[]{:S(2)}) copy-start(bf16[80,1664]{1,0:T(8,128)(2,1)S(1)} %collective-permute-done.5.refs_6_) | copy-start | bytes 798724
  32.9 1.5 %copy-start.8 = (bf16[80,1664]{1,0:T(8,128)(2,1)}, bf16[80,1664]{1,0:T(8,128)(2,1)S(1)}, u32[]{:S(2)}) copy-start(bf16[80,1664]{1,0:T(8,128)(2,1)S(1)} %collective-permute-done.4.refs_5_) | copy-start | bytes 798724
  34.3 0.7 copy-start.9
  70.6 8.1 %collective-permute-start.9 = (bf16[784,128]{1,0:T(8,128)(2,1)}, bf16[784,128]{1,0:T(8,128)(2,1)S(1)}, u32[]{:S(2)}, u32[]{:S(2)}) collective-permute-start(bf16[784,128]{1,0:T(8,128)(2,1)} %get-tuple-element.9), channel_id=1, source_target_pairs={{0,8},{8,0},{16,24},{24,16},{1,9},{9,1},{17,25},{25,17},{2,10},{10... | collective-permute-start | bytes 602120 | tf_op jit(solution)/shard_map/ppermute | solution.py:843
  72.2 11.3 %collective-permute-start.10 = (bf16[784,128]{1,0:T(8,128)(2,1)}, bf16[784,128]{1,0:T(8,128)(2,1)S(1)}, u32[]{:S(2)}, u32[]{:S(2)}) collective-permute-start(bf16[784,128]{1,0:T(8,128)(2,1)} %get-tuple-element.10), channel_id=1, source_target_pairs={{0,16},{8,24},{16,0},{24,8},{1,17},{9,25},{17,1},{25,9},{2,18},{10... | collective-permute-start | bytes 602120 | tf_op jit(solution)/shard_map/ppermute | solution.py:843
  73.7 9.8 %collective-permute-start.11 = (bf16[784,128]{1,0:T(8,128)(2,1)}, bf16[784,128]{1,0:T(8,128)(2,1)S(1)}, u32[]{:S(2)}, u32[]{:S(2)}) collective-permute-start(bf16[784,128]{1,0:T(8,128)(2,1)} %get-tuple-element.11), channel_id=1, source_target_pairs={{0,24},{8,16},{16,8},{24,0},{1,25},{9,17},{17,9},{25,1},{2,26},{10... | collective-permute-start | bytes 602120 | tf_op jit(solution)/shard_map/ppermute | solution.py:843
  83.5 0.9 %copy-start = (bf16[784,128]{1,0:T(8,128)(2,1)S(1)}, bf16[784,128]{1,0:T(8,128)(2,1)}, u32[]{:S(2)}) copy-start(bf16[784,128]{1,0:T(8,128)(2,1)} %get-tuple-element.8.refs_0_) | copy-start | bytes 602116
